TPU v7x, 32 devices: a whole 2x2x4 slice. The times are simulated.
32 devices in a mesh: gx: 4 (over x, core), gy: 8 (over z, y).
Axes of the slice: x: 2, y: 2, z: 4, core: 2. Of those that a mesh axis runs over, the one named last changes fastest.
Arguments:
- features: bfloat16 [32, 64, 96, 128], P('gx', 'gy'), may hold values from -6 to 6
- active_mask: int32 [32, 64, 128], P('gx', 'gy'), may hold values 0 or 1
- owners: int32 [4, 8, 16], P('gx', 'gy'), may hold values from 0 to 7, as said below
- weight: bfloat16 [3, 3, 96, 288], replicated, may hold values from -0.125 to 0.125
- channel_bias: float32 [96], replicated, may hold values from -3 to 3
- cotangent: bfloat16 [4, 256, 96, 512], P('gx', 'gy'), may hold values from -6 to 6
Outputs:
- activations: bfloat16 [4, 256, 96, 512], P('gx', 'gy')
- grad_features: bfloat16 [32, 64, 96, 128], P('gx', 'gy')
- grad_weight: float32 [3, 3, 96, 288], replicated
Inputs may be any that keep to these rules, and one draw needn't show every extreme that they name: `owners`: of the bricks of one tile at most 4 have the same owner, and in every gx row one owner receives exactly 4 bricks from every tile of the row.
All inputs are finite; a program needn't handle non-finite values. No bound on the sum of `active_mask` on one device may be relied on, other than what follows from the above.
Results may differ from a plain program's by a relative error of at most 0.005.
Values may be sent and summed in bfloat16 or wider, within the bound.
No kernel may reach another device: no remote copies, remote signals or barrier semaphores. Data moves between devices by JAX's collectives and lax.ppermute only.
A program may use at most 320 MiB of HBM per device.

v0:
```python
import jax
import jax.numpy as jnp
from jax import lax
from jax.sharding import PartitionSpec as P


def padded_2(block, sides, width):
    for axis, dim in sides:
        count = lax.axis_size(axis)
        forward = [(i, i + 1) for i in range(count - 1)]
        backward = [(target, source) for source, target in forward]
        low = lax.ppermute(
            lax.slice_in_dim(block, block.shape[dim] - width, None, axis=dim), axis, forward
        )
        high = lax.ppermute(lax.slice_in_dim(block, 0, width, axis=dim), axis, backward)
        block = jnp.concatenate([low, block, high], axis=dim)
    return block


def scene_bricks(volume):
    across, column, channels = (volume.shape[1], volume.shape[3], volume.shape[2])
    reshaped = volume.reshape(8, across // 8, 8, channels, column // 8, 8)
    reshaped = jnp.transpose(reshaped, (1, 4, 3, 0, 2, 5))
    return reshaped.reshape(across // 8 * (column // 8), channels, 512)


def brick_scene(bricks, across, column):
    channels = bricks.shape[1]
    reshaped = bricks.reshape(across // 8, column // 8, channels, 8, 8, 8)
    reshaped = jnp.transpose(reshaped, (3, 0, 4, 2, 1, 5))
    return reshaped.reshape(8, across, channels, column)


def slot_table(owners, members, capacity):
    owner_list = owners.reshape(-1)
    matches = (owner_list[:, None] == jnp.arange(members, dtype=jnp.int32)[None, :]).astype(
        jnp.int32
    )
    before = jnp.cumsum(matches, axis=0) - matches
    ranking = jnp.sum(before * matches, axis=1)
    target = owner_list * capacity + ranking
    return (target[:, None] == jnp.arange(members * capacity, dtype=jnp.int32)[None, :]).astype(
        jnp.bfloat16
    )


def stack_depth(padded):
    column = padded.shape[3]
    deeper = jnp.pad(padded, ((0, 0), (0, 0), (0, 0), (1, 1)))
    return jnp.concatenate(
        [deeper[..., 0:column], deeper[..., 1 : column + 1], deeper[..., 2 : column + 2]], axis=2
    )


def conv_taps(stacked, kernel):
    rows_x = stacked.shape[0] - 2
    rows_y = stacked.shape[1] - 2
    summed = jnp.zeros((rows_x, rows_y, kernel.shape[2], stacked.shape[3]), jnp.float32)
    for shift_x in range(3):
        for shift_y in range(3):
            summed = summed + jnp.einsum(
                "oc,xycz->xyoz",
                kernel[shift_x, shift_y],
                stacked[shift_x : shift_x + rows_x, shift_y : shift_y + rows_y],
                preferred_element_type=jnp.float32,
            )
    return summed


def on_device(features, active_mask, owners, weight, channel_bias, cotangent):
    across = features.shape[1]
    channels = features.shape[2]
    column = features.shape[3]
    members = lax.axis_size("gy")
    bricks_dev = owners.size
    capacity = max(2, 2 * bricks_dev // members)
    slot_count = members * capacity
    active_half = active_mask.astype(jnp.bfloat16)[:, :, None, :]
    active = active_mask.astype(jnp.float32)[:, :, None, :]
    masked_input = features * active_half
    padded = padded_2(masked_input, (("gx", 0), ("gy", 1)), 1)
    stacked = stack_depth(padded)
    routing = slot_table(owners, members, capacity)
    own_cotangent = cotangent.reshape(members, capacity, channels, 512)
    preact = conv_taps(stacked, weight) + channel_bias[None, None, :, None]
    gating = jax.nn.sigmoid(preact)
    activated_scene = (active * preact * gating).astype(jnp.bfloat16)
    outgoing = jnp.einsum(
        "bs,bcv->scv", routing, scene_bricks(activated_scene), preferred_element_type=jnp.float32
    ).astype(jnp.bfloat16)
    outgoing = outgoing.reshape(members, capacity, channels, 512)
    activations = lax.all_to_all(outgoing, "gy", split_axis=0, concat_axis=0, tiled=True).reshape(
        1, slot_count, channels, 512
    )
    returned = lax.all_to_all(own_cotangent, "gy", split_axis=0, concat_axis=0, tiled=True)
    cotan_bricks = jnp.einsum(
        "bs,scv->bcv",
        routing,
        returned.reshape(slot_count, channels, 512),
        preferred_element_type=jnp.float32,
    ).astype(jnp.bfloat16)
    cotangent_scene = brick_scene(cotan_bricks, across, column)
    slope = (
        cotangent_scene.astype(jnp.float32) * active * gating * (1.0 + preact * (1.0 - gating))
    ).astype(jnp.bfloat16)
    slope_padded = padded_2(slope, (("gx", 0), ("gy", 1)), 1)
    mirror = jnp.transpose(
        weight.reshape(3, 3, channels, 3, channels)[::-1, ::-1, :, ::-1, :], (0, 1, 4, 3, 2)
    ).reshape(3, 3, channels, 3 * channels)
    grad_inner = conv_taps(stack_depth(slope_padded), mirror)
    grad_features = (active * grad_inner).astype(jnp.bfloat16)
    tap_rows = []
    for shift_x in range(3):
        tap_row = []
        for shift_y in range(3):
            tap_row.append(
                jnp.einsum(
                    "xyoz,xycz->oc",
                    slope,
                    stacked[shift_x : shift_x + 8, shift_y : shift_y + across],
                    preferred_element_type=jnp.float32,
                )
            )
        tap_rows.append(jnp.stack(tap_row))
    tap_sums = jnp.stack(tap_rows)
    voxel_total = 8 * across * column * lax.axis_size("gx") * members
    grad_weight = lax.psum(tap_sums, ("gx", "gy")) * voxel_total ** (-0.5)
    return (activations, grad_features, grad_weight)


def solution(mesh):
    in_specs = (
        P("gx", "gy", None, None),
        P("gx", "gy", None),
        P("gx", "gy", None),
        P(),
        P(),
        P("gx", "gy", None, None),
    )
    out_specs = (P("gx", "gy", None, None), P("gx", "gy", None, None), P())
    return jax.shard_map(
        on_device, mesh=mesh, in_specs=in_specs, out_specs=out_specs, check_vma=False
    )
```

profile of v0, /device:TPU:11, one launch (start us, length us, event | category | flops | bytes accessed | tf_op | source)
XLA Modules:
  0.0 384.5 jit_solution(6761306423937400518)
XLA Ops:
  12.2 3.2 collective-permute-start.1
  15.5 4.1 %copy.57 = bf16[8,4,96,512]{3,1,2,0:T(4,128)(2,1)} copy(bf16[8,4,96,512]{3,2,1,0:T(8,128)(2,1)S(1)} %bitcast.270) | data formatting | bytes 6291456 | tf_op jit(solution)/shard_map/reshape | solution.py:84
  19.6 5.9 %all-to-all-start.1 = ((bf16[8,4,96,512]{3,1,2,0:T(4,128)(2,1)}), bf16[8,4,96,512]{3,1,2,0:T(4,128)(2,1)}, u32[]{:S(2)}, u32[]{:S(2)}) async-start(bf16[8,4,96,512]{3,1,2,0:T(4,128)(2,1)} %copy.57), calls=%async_computation.1 | async-start | bytes 6291456 | tf_op jit(solution)/shard_map/all_to_all | solution.py:95
  28.7 3.1 collective-permute-start.2
  31.8 3.3 collective-permute-start.3
  36.4 46.1 %collective-permute-done.2 = bf16[10,1,96,128]{3,2,1,0:T(8,128)(2,1)S(1)} collective-permute-done((bf16[10,1,96,128]{3,2,1,0:T(8,128)(2,1)}, bf16[10,1,96,128]{3,2,1,0:T(8,128)(2,1)S(1)}, u32[]{:S(2)}, u32[]{:S(2)}) %collective-permute-start.2) | collective-permute-done | bytes 245792 | tf_op jit(solution)/shard_map/ppermute | solution.py:12
  82.4 5.4 %select_maximum_fusion.4 = bf16[10,10,96,130]{3,2,1,0:T(8,128)(2,1)S(1)} fusion(bf16[10,1,96,128]{3,2,1,0:T(8,128)(2,1)} %collective-permute-done.3, bf16[10,1,96,128]{3,2,1,0:T(8,128)(2,1)S(1)} %collective-permute-done.2, bf16[1,8,96,128]{3,2,1,0:T(8,128)(2,1)S(1)} %collective-permute-done.1, bf16[8,8,96,128]{3,2,1,0:T(8,128)(2,1)S(1)} %broadcast_multiply_fusion, ...), kind=kLoop, calls=%fused_computation.9 | loop fusion | flops 22464000 | bytes 4953600 | tf_op jit(solution)/shard_map/concatenate | solution.py:16
  89.1 4.5 %pad_maximum_fusion = bf16[10,10,288,128]{3,2,1,0:T(8,128)(2,1)S(1)} fusion(bf16[10,10,96,128]{3,2,1,0:T(8,128)(2,1)S(1)} %get-tuple-element.6, bf16[10,1,96,128]{3,2,1,0:T(8,128)(2,1)} %collective-permute-done.3, bf16[1,8,96,128]{3,2,1,0:T(8,128)(2,1)S(1)} %collective-permute-done.1, bf16[8,8,96,128]{3,2,1,0:T(8,128)(2,1)S(1)} %broadcast_multiply_fusion, ...), kind=kLoop, calls=%fused_computation.3 | loop fusion | flops 51609600 | bytes 14745600 | tf_op jit(solution)/shard_map/concatenate | solution.py:50
  93.7 3.4 fusion.30
  97.1 3.0 fusion.34
  100.1 3.0 fusion.38
  103.1 3.0 fusion.42
  106.1 3.0 fusion.46
  109.0 2.9 fusion.50
  111.9 2.9 fusion.54
  114.9 3.0 fusion.58
  117.9 3.6 copy.58
  121.5 3.3 reshape.57
  124.8 2.5 fusion.68
  127.4 3.3 copy.59
  130.6 4.7 %copy.110 = f32[8,1,8,96,16,8]{3,5,4,2,0,1:T(8,128)} copy(f32[8,1,8,96,16,8]{3,5,2,0,4,1:T(8,128)} %bitcast.266) | data formatting | bytes 6291456 | tf_op jit(solution)/shard_map/convert_element_type | solution.py:104
  135.4 5.4 %copy.61 = f32[8,8,96,128]{3,2,1,0:T(8,128)} copy(f32[8,8,96,128]{2,3,1,0:T(8,128)} %bitcast.267) | data formatting | bytes 6291456 | tf_op jit(solution)/shard_map/convert_element_type | solution.py:104
  140.7 14.8 %fusion.67 = (bf16[8,8,96,128]{3,2,1,0:T(8,128)(2,1)S(1)}, bf16[8,8,96,128]{3,2,1,0:T(8,128)(2,1)}) fusion(f32[8,8,96,128]{3,2,1,0:T(8,128)} %copy.61, f32[8,8,128]{2,1,0:T(8,128)S(1)} %copy-done.7, f32[96]{0:T(128)S(1)} %copy-done.10, bf16[10,10,288,128]{3,2,1,0:T(8,128)(2,1)} %copy-done, bf16[3,3,96,288]{3,2,1,0:T(8,128)(2,1)} %param.9, ...), kind=kOutput, calls=%fused_computation.81 | convolution fusion | flops 470286336 | bytes 36282752 | tf_op jit(solution)/shard_map/oc,xycz->xyoz/dot_general | solution.py:61
  160.8 1.8 fusion.85
  164.4 1.8 fusion.79
  166.1 1.8 fusion.76
  173.5 8.2 %collective-permute-start.5 = (bf16[1,8,96,128]{3,2,1,0:T(8,128)(2,1)}, bf16[1,8,96,128]{3,2,1,0:T(8,128)(2,1)S(1)}, u32[]{:S(2)}, u32[]{:S(2)}) collective-permute-start(bf16[1,8,96,128]{3,2,1,0:T(8,128)(2,1)} %get-tuple-element.14), channel_id=1, source_target_pairs={{8,0},{16,8},{24,16},{9,1},{17,9},{25,17},{10,2},{18,10},{26,18},{... | collective-permute-start | bytes 589832 | tf_op jit(solution)/shard_map/ppermute | solution.py:15
  183.1 3.0 copy.52
  186.1 3.7 copy.53
  189.7 3.2 copy.54
  193.8 16.3 %collective-permute-start.6 = (bf16[10,1,96,128]{3,2,1,0:T(8,128)(2,1)}, bf16[10,1,96,128]{3,2,1,0:T(8,128)(2,1)}, u32[]{:S(2)}, u32[]{:S(2)}) collective-permute-start(bf16[10,1,96,128]{3,2,1,0:T(8,128)(2,1)} %get-tuple-element.9), channel_id=1, source_target_pairs={{0,1},{1,2},{2,3},{3,4},{4,5},{5,6},{6,7},{8,9},{9,10},{10,11},{11... | collective-permute-start | bytes 737288 | tf_op jit(solution)/shard_map/ppermute | solution.py:12
  210.1 1.9 collective-permute-start.7
  212.0 2.8 convolution_convert_fusion
  214.8 5.5 %reshape.54 = bf16[8,4,96,512]{3,1,0,2:T(4,128)(2,1)} reshape(bf16[32,96,512]{2,0,1:T(8,128)(2,1)} %convolution_convert_fusion) | data formatting | bytes 6291456 | tf_op jit(solution)/shard_map/reshape | solution.py:91
  220.3 4.7 %copy.55 = bf16[8,4,96,512]{3,1,2,0:T(4,128)(2,1)} copy(bf16[8,4,96,512]{3,1,0,2:T(4,128)(2,1)} %reshape.54) | data formatting | bytes 6291456 | tf_op jit(solution)/shard_map/reshape | solution.py:91
  225.0 4.6 %all-to-all-start = ((bf16[8,4,96,512]{3,1,2,0:T(4,128)(2,1)}), bf16[8,4,96,512]{3,1,2,0:T(4,128)(2,1)}, u32[]{:S(2)}, u32[]{:S(2)}) async-start(bf16[8,4,96,512]{3,1,2,0:T(4,128)(2,1)} %copy.55), calls=%async_computation | async-start | bytes 6291456 | tf_op jit(solution)/shard_map/all_to_all | solution.py:92
  229.6 5.5 %select_maximum_fusion = bf16[10,10,96,130]{3,2,1,0:T(8,128)(2,1)S(1)} fusion(bf16[10,1,96,128]{3,2,1,0:T(8,128)(2,1)} %collective-permute-done.7, bf16[10,1,96,128]{3,2,1,0:T(8,128)(2,1)} %collective-permute-done.6, bf16[1,8,96,128]{3,2,1,0:T(8,128)(2,1)S(1)} %collective-permute-done.5, bf16[8,8,96,128]{3,2,1,0:T(8,128)(2,1)S(1)} %copy-done.2, ...), kind=kLoop, calls=%fused_computation.5 | loop fusion | flops 22464000 | bytes 4953600 | tf_op jit(solution)/shard_map/concatenate | solution.py:16
  236.4 4.7 %pad_maximum_fusion.1 = bf16[10,10,288,128]{3,2,1,0:T(8,128)(2,1)S(1)} fusion(bf16[10,10,96,128]{3,2,1,0:T(8,128)(2,1)S(1)} %get-tuple-element.4, bf16[10,1,96,128]{3,2,1,0:T(8,128)(2,1)} %collective-permute-done.7, bf16[1,8,96,128]{3,2,1,0:T(8,128)(2,1)S(1)} %collective-permute-done.5, bf16[8,8,96,128]{3,2,1,0:T(8,128)(2,1)S(1)} %copy-done.2, ...), kind=kLoop, calls=%fused_computation.4 | loop fusion | flops 51609600 | bytes 14745600 | tf_op jit(solution)/shard_map/concatenate | solution.py:50
  243.6 2.9 fusion.12
  246.5 3.0 fusion.14
  249.5 2.9 fusion.16
  252.4 2.9 fusion.18
  255.3 2.9 fusion.20
  258.2 2.9 fusion.22
  261.2 9.2 %fusion.69 = bf16[8,8,96,128]{3,2,1,0:T(8,128)(2,1)} fusion(f32[8,8,128,96]{2,3,1,0:T(8,128)S(1)} %fusion.8, f32[8,8,128,96]{2,3,1,0:T(8,128)S(1)} %fusion.10, f32[8,8,128,96]{2,3,1,0:T(8,128)} %fusion.12, f32[8,8,128,96]{2,3,1,0:T(8,128)} %fusion.14, f32[8,8,128,96]{2,3,1,0:T(8,128)} %fusion.16, f32[8,8,128,96]{2,3,1,0:T(8,128)} %fusion.18, ...), kind=kOutput, calls=%fused_computation.87 | convolution fusion | flops 460849152 | bytes 31563776 | tf_op jit(solution)/shard_map/oc,xycz->xyoz/dot_general | solution.py:61
  270.3 100.3 %all-reduce.4.cloned.1.call-done = f32[3,3,96,288]{3,2,1,0:T(8,128)} async-done(((f32[3,3,96,288]{3,2,1,0:T(8,128)}), f32[3,3,96,288]{3,2,1,0:T(8,128)}) %all-reduce.4.cloned.1.call-update) | async-done | bytes 995344 | tf_op jit(solution)/shard_map/psum | solution.py:127
  370.6 2.5 broadcast_multiply_fusion.1
  373.1 4.4 %copy.56 = bf16[8,4,96,512]{3,2,1,0:T(8,128)(2,1)} copy(bf16[8,4,96,512]{3,1,2,0:T(4,128)(2,1)} %all-to-all-done) | data formatting | bytes 6291456 | tf_op jit(solution)/shard_map/all_to_all | solution.py:92
  (66 shorter events, 29.4 us)
Async XLA Ops:
  7.2 8.3 %copy-start.4 = (bf16[1,32,96,512]{3,2,1,0:T(8,128)(2,1)S(1)}, bf16[1,32,96,512]{3,2,1,0:T(8,128)(2,1)}, u32[]{:S(2)}) copy-start(bf16[1,32,96,512]{3,2,1,0:T(8,128)(2,1)} %param.11) | copy-start | bytes 9437188
  10.9 16.9 %collective-permute-start = (bf16[1,8,96,128]{3,2,1,0:T(8,128)(2,1)}, bf16[1,8,96,128]{3,2,1,0:T(8,128)(2,1)S(1)}, u32[]{:S(2)}, u32[]{:S(2)}) collective-permute-start(bf16[1,8,96,128]{3,2,1,0:T(8,128)(2,1)} %get-tuple-element.15), channel_id=1, source_target_pairs={{0,8},{8,16},{16,24},{1,9},{9,17},{17,25},{2,10},{10,18},{18,26},{... | collective-permute-start | bytes 589832 | tf_op jit(solution)/shard_map/ppermute | solution.py:12
  12.2 15.6 %collective-permute-start.1 = (bf16[1,8,96,128]{3,2,1,0:T(8,128)(2,1)S(1)}, bf16[1,8,96,128]{3,2,1,0:T(8,128)(2,1)S(1)}, u32[]{:S(2)}, u32[]{:S(2)}) collective-permute-start(bf16[1,8,96,128]{3,2,1,0:T(8,128)(2,1)S(1)} %get-tuple-element.16), channel_id=1, source_target_pairs={{8,0},{16,8},{24,16},{9,1},{17,9},{25,17},{10,2},{18,10},{26,18},{... | collective-permute-start | bytes 589832 | tf_op jit(solution)/shard_map/ppermute | solution.py:15
  19.6 5.9 %copy-start.9 = (s32[1,1,16]{2,1,0:T(1,128)S(1)}, s32[1,1,16]{2,1,0:T(1,128)}, u32[]{:S(2)}) copy-start(s32[1,1,16]{2,1,0:T(1,128)} %param.8) | copy-start | bytes 196
  19.6 5.9 %copy-start.5 = (bf16[3,3,96,288]{3,2,1,0:T(8,128)(2,1)S(1)}, bf16[3,3,96,288]{3,2,1,0:T(8,128)(2,1)}, u32[]{:S(2)}) copy-start(bf16[3,3,96,288]{3,2,1,0:T(8,128)(2,1)} %param.9) | copy-start | bytes 1492996
  19.6 98.3 %all-to-all-start.1 = ((bf16[8,4,96,512]{3,1,2,0:T(4,128)(2,1)}), bf16[8,4,96,512]{3,1,2,0:T(4,128)(2,1)}, u32[]{:S(2)}, u32[]{:S(2)}) async-start(bf16[8,4,96,512]{3,1,2,0:T(4,128)(2,1)} %copy.57), calls=%async_computation.1 | async-start | bytes 6291456 | tf_op jit(solution)/shard_map/all_to_all | solution.py:95
  25.4 345.2 %all-reduce.4.cloned.1.call-start = ((), (), s32[]{:S(2)}) async-start(), calls=%async_computation.2 | async-start | bytes 2654208 | tf_op jit(solution)/shard_map/psum | solution.py:127
  28.7 53.8 %collective-permute-start.2 = (bf16[10,1,96,128]{3,2,1,0:T(8,128)(2,1)}, bf16[10,1,96,128]{3,2,1,0:T(8,128)(2,1)S(1)}, u32[]{:S(2)}, u32[]{:S(2)}) collective-permute-start(bf16[10,1,96,128]{3,2,1,0:T(8,128)(2,1)} %get-tuple-element.11), channel_id=1, source_target_pairs={{0,1},{1,2},{2,3},{3,4},{4,5},{5,6},{6,7},{8,9},{9,10},{10,11},{11... | collective-permute-start | bytes 737288 | tf_op jit(solution)/shard_map/ppermute | solution.py:12
  31.8 50.7 %collective-permute-start.3 = (bf16[10,1,96,128]{3,2,1,0:T(8,128)(2,1)}, bf16[10,1,96,128]{3,2,1,0:T(8,128)(2,1)}, u32[]{:S(2)}, u32[]{:S(2)}) collective-permute-start(bf16[10,1,96,128]{3,2,1,0:T(8,128)(2,1)} %get-tuple-element.12), channel_id=1, source_target_pairs={{1,0},{2,1},{3,2},{4,3},{5,4},{6,5},{7,6},{9,8},{10,9},{11,10},{12... | collective-permute-start | bytes 737288 | tf_op jit(solution)/shard_map/ppermute | solution.py:15
  93.7 21.2 %copy-start = (bf16[10,10,288,128]{3,2,1,0:T(8,128)(2,1)}, bf16[10,10,288,128]{3,2,1,0:T(8,128)(2,1)S(1)}, u32[]{:S(2)}) copy-start(bf16[10,10,288,128]{3,2,1,0:T(8,128)(2,1)S(1)} %pad_maximum_fusion) | copy-start | bytes 22118404
  135.3 5.4 %copy-start.7 = (f32[8,8,128]{2,1,0:T(8,128)S(1)}, f32[8,8,128]{2,1,0:T(8,128)}, u32[]{:S(2)}) copy-start(f32[8,8,128]{2,1,0:T(8,128)} %get-tuple-element.17) | copy-start | bytes 98308
  135.4 5.4 %copy-start.10 = (f32[96]{0:T(128)S(1)}, f32[96]{0:T(128)}, u32[]{:S(2)}) copy-start(f32[96]{0:T(128)} %param.10) | copy-start | bytes 1156
  135.4 20.2 %slice-start = ((s8[7372800]{0:T(1024)(128)(4,1)}), s8[3178496]{0:T(1024)(128)(4,1)S(1)}, s32[]{:S(2)}) async-start(s8[7372800]{0:T(1024)(128)(4,1)} %bitcast.264), calls=%async_computation.3 | async-start | bytes 6356992
  140.7 14.8 %slice-start.1 = ((s8[7372800]{0:T(1024)(128)(4,1)}), s8[4194304]{0:T(1024)(128)(4,1)S(1)}, s32[]{:S(2)}) async-start(s8[7372800]{0:T(1024)(128)(4,1)} %bitcast.264), calls=%async_computation.4 | async-start | bytes 8388608
  155.5 15.9 %copy-start.1 = (bf16[8,8,96,128]{3,2,1,0:T(8,128)(2,1)}, bf16[8,8,96,128]{3,2,1,0:T(8,128)(2,1)S(1)}, u32[]{:S(2)}) copy-start(bf16[8,8,96,128]{3,2,1,0:T(8,128)(2,1)S(1)} %get-tuple-element.7) | copy-start | bytes 4718596
  171.4 11.6 %copy-start.3 = (bf16[8,8,96,128]{3,2,1,0:T(8,128)(2,1)S(1)}, bf16[8,8,96,128]{3,2,1,0:T(8,128)(2,1)}, u32[]{:S(2)}) copy-start(bf16[8,8,96,128]{3,2,1,0:T(8,128)(2,1)} %get-tuple-element.8) | copy-start | bytes 4718596
  172.2 20.7 %collective-permute-start.4 = (bf16[1,8,96,128]{3,2,1,0:T(8,128)(2,1)}, bf16[1,8,96,128]{3,2,1,0:T(8,128)(2,1)S(1)}, u32[]{:S(2)}, u32[]{:S(2)}) collective-permute-start(bf16[1,8,96,128]{3,2,1,0:T(8,128)(2,1)} %get-tuple-element.13), channel_id=1, source_target_pairs={{0,8},{8,16},{16,24},{1,9},{9,17},{17,25},{2,10},{10,18},{18,26},{... | collective-permute-start | bytes 589832 | tf_op jit(solution)/shard_map/ppermute | solution.py:12
  173.5 19.4 %collective-permute-start.5 = (bf16[1,8,96,128]{3,2,1,0:T(8,128)(2,1)}, bf16[1,8,96,128]{3,2,1,0:T(8,128)(2,1)S(1)}, u32[]{:S(2)}, u32[]{:S(2)}) collective-permute-start(bf16[1,8,96,128]{3,2,1,0:T(8,128)(2,1)} %get-tuple-element.14), channel_id=1, source_target_pairs={{8,0},{16,8},{24,16},{9,1},{17,9},{25,17},{10,2},{18,10},{26,18},{... | collective-permute-start | bytes 589832 | tf_op jit(solution)/shard_map/ppermute | solution.py:15
  186.0 6.9 %copy-start.2 = (bf16[8,8,96,128]{3,2,1,0:T(8,128)(2,1)S(1)}, bf16[8,8,96,128]{3,2,1,0:T(8,128)(2,1)}, u32[]{:S(2)}) copy-start(bf16[8,8,96,128]{3,2,1,0:T(8,128)(2,1)} %copy-done.1) | copy-start | bytes 4718596
  193.8 35.8 %collective-permute-start.6 = (bf16[10,1,96,128]{3,2,1,0:T(8,128)(2,1)}, bf16[10,1,96,128]{3,2,1,0:T(8,128)(2,1)}, u32[]{:S(2)}, u32[]{:S(2)}) collective-permute-start(bf16[10,1,96,128]{3,2,1,0:T(8,128)(2,1)} %get-tuple-element.9), channel_id=1, source_target_pairs={{0,1},{1,2},{2,3},{3,4},{4,5},{5,6},{6,7},{8,9},{9,10},{10,11},{11... | collective-permute-start | bytes 737288 | tf_op jit(solution)/shard_map/ppermute | solution.py:12
  210.1 19.6 %collective-permute-start.7 = (bf16[10,1,96,128]{3,2,1,0:T(8,128)(2,1)}, bf16[10,1,96,128]{3,2,1,0:T(8,128)(2,1)}, u32[]{:S(2)}, u32[]{:S(2)}) collective-permute-start(bf16[10,1,96,128]{3,2,1,0:T(8,128)(2,1)} %get-tuple-element.10), channel_id=1, source_target_pairs={{1,0},{2,1},{3,2},{4,3},{5,4},{6,5},{7,6},{9,8},{10,9},{11,10},{12... | collective-permute-start | bytes 737288 | tf_op jit(solution)/shard_map/ppermute | solution.py:15
  225.0 148.1 %all-to-all-start = ((bf16[8,4,96,512]{3,1,2,0:T(4,128)(2,1)}), bf16[8,4,96,512]{3,1,2,0:T(4,128)(2,1)}, u32[]{:S(2)}, u32[]{:S(2)}) async-start(bf16[8,4,96,512]{3,1,2,0:T(4,128)(2,1)} %copy.55), calls=%async_computation | async-start | bytes 6291456 | tf_op jit(solution)/shard_map/all_to_all | solution.py:92
  236.4 4.7 %copy-start.6 = (bf16[3,3,96,3,96]{2,4,3,1,0:T(8,128)(2,1)S(1)}, bf16[3,3,96,3,96]{2,4,3,1,0:T(8,128)(2,1)}, u32[]{:S(2)}) copy-start(bf16[3,3,96,3,96]{2,4,3,1,0:T(8,128)(2,1)} %copy.63) | copy-start | bytes 1492996
  258.2 2.9 copy-start.8
Sparse Core Ops, SparseCore 0:
  183.2 187.3 all-reduce.3
where the time goes:
time: 391 us; the launch traced here: 384 us
  waiting for transfers between devices  146 us (37%)
  matrix products  89.2 us (23%)
  local copies, waits for them, and re-layouts  56.4 us (14%)
  starting transfers between devices  49 us (13%)
  other arithmetic  28.9 us (7%)
  between operations  14.6 us (4%)
    psum x1, waiting for transfers between devices, on_device(): grad_weight = lax.psum(tap_sums, ('gx', 'gy')) * voxel_total ** (-0.5)  100 us
    dot_general x18, matrix products, conv_taps(): jnp.einsum('oc,xycz->xyoz', kernel[shift_x, shift_y], stacked[shift_x:shi...  68.1 us
    ppermute x4, waiting for transfers between devices, padded_2(): lax.ppermute(lax.slice_in_dim(block, block.shape[dim] - width, None, axis...  46.1 us
    ppermute x4, starting transfers between devices, padded_2(): lax.ppermute(lax.slice_in_dim(block, block.shape[dim] - width, None, axis...  21.9 us
    ppermute x4, starting transfers between devices, padded_2(): lax.ppermute(lax.slice_in_dim(block, 0, width, axis=dim), axis, backward)  16.6 us
    dot_general x9, matrix products, on_device(): jnp.einsum('xyoz,xycz->oc', slope, stacked[shift_x:shift_x + 8, shift_y:s...  15.8 us
    convert_element_type x3, local copies, waits for them, and re-layouts, on_device(): cotangent_scene.astype(jnp.float32) * active * gating  13.4 us
    concatenate x2, other arithmetic, padded_2(): block = jnp.concatenate([low, block, high], axis=dim)  10.9 us
  transfers between devices with their start and end apart: 11, of which 2 were waited for; matrix products, arithmetic and copies ran while one was open for 29% of the time, Pallas kernels for 0%

commit v1 on v0

v1 whole, which is shorter than its diff:
```python
import functools

import jax
import jax.numpy as jnp
from jax import lax
from jax.experimental import pallas as pl
from jax.experimental.pallas import tpu as pltpu
from jax.sharding import PartitionSpec as P

BRICK = 8
LANES = 128
GROUP = LANES // BRICK
CHUNK = 32
VMEM_LIMIT = 48 * 2**20


def shift_lanes(value, by):
    width = value.shape[-1]
    lane = lax.broadcasted_iota(jnp.int32, value.shape, value.ndim - 1)
    rolled = pltpu.roll(value, by % width, value.ndim - 1)
    inside = lane >= by if by > 0 else lane < width + by
    return jnp.where(inside, rolled, jnp.zeros_like(rolled))


def swap_blocks(tiles):
    axis = tiles[0].ndim - 1
    block = lax.broadcasted_iota(jnp.int32, tiles[0].shape, axis) // BRICK
    turned = []
    for k in range(GROUP):
        source = -k % GROUP
        tile = tiles[source]
        turned.append(pltpu.roll(tile, BRICK * source, axis) if source else tile)
    step = 1
    while step < GROUP:
        moved = (block // step) % 2 == 1
        turned = [
            jnp.where(moved, turned[(k - step) % GROUP], turned[k]) for k in range(GROUP)
        ]
        step *= 2
    return [
        pltpu.roll(turned[k], LANES - BRICK * k, axis) if k else turned[k] for k in range(GROUP)
    ]


def fill_slots(me_ref, owners_ref, slots_ref, counts_ref, capacity):
    def clear(member, carry):
        counts_ref[member] = 0
        return carry

    lax.fori_loop(0, counts_ref.shape[0], clear, 0)

    def place(brick, carry):
        owner = owners_ref[brick]
        rank = counts_ref[owner]
        slots_ref[brick] = (owner ^ me_ref[0]) * capacity + rank
        counts_ref[owner] = rank + 1
        return carry

    lax.fori_loop(0, slots_ref.shape[0], place, 0)


def copy_all(pairs, sems):
    copies = [
        pltpu.make_async_copy(source, target, sems.at[i])
        for i, (source, target) in enumerate(pairs)
    ]
    for copy in copies:
        copy.start()
    return copies


def columns_of(ref, row, across):
    return jnp.concatenate(
        [ref[row + dx, across + dy] for dx in range(3) for dy in range(3)], axis=0
    )


def conv_two(kernel, ref, row, across):
    channels = ref.shape[2]
    stacked = jnp.concatenate(
        [columns_of(ref, row, across), columns_of(ref, row, across + 1)], axis=1
    )
    product = jnp.dot(kernel, stacked, preferred_element_type=jnp.float32)
    results = []
    for half in range(2):
        part = product[:, half * LANES : (half + 1) * LANES]
        results.append(
            shift_lanes(part[:channels], 1)
            + part[channels : 2 * channels]
            + shift_lanes(part[2 * channels :], -1)
        )
    return results


def fill_padded(padded_ref, y_low, y_high, x_low, x_high):
    rows, across = padded_ref.shape[0] - 2, padded_ref.shape[1] - 2
    for y in range(across + 2):
        padded_ref[0, y] = x_low[0, y]
        padded_ref[rows + 1, y] = x_high[0, y]
    for x in range(rows):
        padded_ref[x + 1, 0] = y_low[x, 0]
        padded_ref[x + 1, across + 1] = y_high[x, 0]


def forward_body(
    members,
    me_ref,
    owners_ref,
    features_ref,
    mask_ref,
    y_low,
    y_high,
    x_low,
    x_high,
    weight_ref,
    bias_ref,
    *refs,
):
    messages, refs = refs[:members], refs[members:]
    padded_ref, factor_ref, backward_ref = refs[:3]
    outgoing_ref, scene_ref, kernel_ref, slots_ref, counts_ref, sems = refs[3:]
    rows, across, channels, _ = features_ref.shape
    capacity = messages[0].shape[0]
    fill_slots(me_ref, owners_ref, slots_ref, counts_ref, capacity)
    fill_padded(padded_ref, y_low, y_high, x_low, x_high)
    for shift in range(3):
        mirrored = slice((2 - shift) * channels, (3 - shift) * channels)
        taken = slice(shift * channels, (shift + 1) * channels)
        for tap in range(9):
            placed = slice(tap * channels, (tap + 1) * channels)
            kernel_ref[taken, placed] = weight_ref[tap, :, taken]
            backward_ref[taken, placed] = weight_ref[8 - tap, :, mirrored].T

    @pl.loop(0, rows)
    def _(x):
        for y in range(across):
            half = mask_ref[x, y : y + 1, :].astype(jnp.float32)
            padded_ref[x + 1, y + 1] = (
                features_ref[x, y].astype(jnp.float32) * half
            ).astype(jnp.bfloat16)

    @pl.loop(0, outgoing_ref.shape[0])
    def _(slot):
        outgoing_ref[slot] = jnp.zeros(outgoing_ref.shape[1:], outgoing_ref.dtype)

    bias = bias_ref[...]

    @pl.loop(0, rows)
    def _(x):
        for y in range(0, across, 2):
            for half, summed in enumerate(conv_two(kernel_ref[...], padded_ref, x, y)):
                preact = summed + bias
                gating = jax.nn.sigmoid(preact)
                active = mask_ref[x, y + half : y + half + 1, :].astype(jnp.float32)
                gated = active * gating
                scene_ref[x * across + y + half] = (preact * gated).astype(scene_ref.dtype)
                factor_ref[x, y + half] = gated * (1.0 + preact * (1.0 - gating))

    for group in range(rows * across // GROUP):

        @pl.loop(0, channels // CHUNK)
        def _(part):
            span = pl.ds(pl.multiple_of(part * CHUNK, CHUNK), CHUNK)
            tiles = swap_blocks([scene_ref[group * GROUP + q, span, :] for q in range(GROUP)])
            for brick in range(GROUP):
                outgoing_ref[
                    slots_ref[brick], span, group * LANES : (group + 1) * LANES
                ] = tiles[brick]

    for copy in copy_all(
        [
            (outgoing_ref.at[k * capacity : (k + 1) * capacity], messages[k])
            for k in range(members)
        ],
        sems,
    ):
        copy.wait()


def slope_body(
    capacity, zero_ref, owners_ref, returned_ref, factor_ref, slope_ref, slots_ref, counts_ref
):
    rows, across, channels, _ = factor_ref.shape
    fill_slots(zero_ref, owners_ref, slots_ref, counts_ref, capacity)
    for group in range(rows * across // GROUP):

        @pl.loop(0, channels // CHUNK)
        def _(part):
            span = pl.ds(pl.multiple_of(part * CHUNK, CHUNK), CHUNK)
            tiles = swap_blocks(
                [
                    returned_ref[
                        slots_ref[brick], span, group * LANES : (group + 1) * LANES
                    ]
                    for brick in range(GROUP)
                ]
            )
            for q in range(GROUP):
                x, y = (group * GROUP + q) // across, (group * GROUP + q) % across
                slope_ref[x, y, span, :] = (
                    tiles[q].astype(jnp.float32) * factor_ref[x, y, span, :]
                ).astype(slope_ref.dtype)


def kernel_grad_body(slope_ref, padded_ref, parts_ref, total_ref):
    rows, across, channels, _ = slope_ref.shape
    total_ref[...] = jnp.zeros_like(total_ref)

    @pl.loop(0, rows)
    def _(x):
        for y in range(0, across, 2):
            shifted = []
            for half in range(2):
                block = slope_ref[x, y + half].astype(jnp.float32)
                shifted.append(
                    jnp.concatenate(
                        [shift_lanes(block, -1), block, shift_lanes(block, 1)], axis=0
                    ).astype(jnp.bfloat16)
                )
            left = jnp.concatenate(shifted, axis=1)
            right = jnp.concatenate(
                [columns_of(padded_ref, x, y), columns_of(padded_ref, x, y + 1)], axis=1
            )
            total_ref[...] += lax.dot_general(
                left, right, (((1,), (1,)), ((), ())), preferred_element_type=jnp.float32
            )

    split, _, share, _ = parts_ref.shape
    for part in range(split):
        for shift in range(3):
            start = shift * channels + part * share
            parts_ref[part, shift] = total_ref[start : start + share, :]


def finish_body(scale, at_ref, *refs):
    pieces, out_ref, shares_ref = refs[:-2], refs[-2], refs[-1]
    split, _, share, _ = shares_ref.shape
    for index, piece in enumerate(pieces):
        shares_ref[at_ref[index]] = piece[...].astype(jnp.float32) * scale
    channels = split * share
    for part in range(split):
        for shift in range(3):
            for tap in range(9):
                out_ref[
                    tap,
                    part * share : (part + 1) * share,
                    shift * channels : (shift + 1) * channels,
                ] = shares_ref[part, shift, :, tap * channels : (tap + 1) * channels]


def features_grad_body(
    slope_ref,
    mask_ref,
    y_low,
    y_high,
    x_low,
    x_high,
    kernel_ref,
    out_ref,
    padded_ref,
):
    rows, across, channels, _ = slope_ref.shape
    fill_padded(padded_ref, y_low, y_high, x_low, x_high)

    @pl.loop(0, rows)
    def _(x):
        for y in range(across):
            padded_ref[x + 1, y + 1] = slope_ref[x, y]

    @pl.loop(0, rows)
    def _(x):
        for y in range(0, across, 2):
            for half, summed in enumerate(conv_two(kernel_ref[...], padded_ref, x, y)):
                active = mask_ref[x, y + half : y + half + 1, :].astype(jnp.float32)
                out_ref[x, y + half] = (active * summed).astype(out_ref.dtype)


def call(body, outs, specs, out_specs, scratch, args, flops, bytes_accessed, transcendentals=0):
    return pl.pallas_call(
        body,
        out_shape=outs,
        in_specs=specs,
        out_specs=out_specs,
        scratch_shapes=scratch,
        compiler_params=pltpu.CompilerParams(vmem_limit_bytes=VMEM_LIMIT),
        cost_estimate=pl.CostEstimate(
            flops=flops, bytes_accessed=bytes_accessed, transcendentals=transcendentals
        ),
    )(*args)


def after(values, *others):
    return lax.optimization_barrier((tuple(values), others))[0]


def from_neighbours(low_edge, high_edge, axis):
    count = lax.axis_size(axis)
    forward = [(i, i + 1) for i in range(count - 1)]
    backward = [(target, source) for source, target in forward]
    return lax.ppermute(high_edge, axis, forward), lax.ppermute(low_edge, axis, backward)


def halo_rows(rows, y_low, y_high):
    pieces = (slice(0, 1), slice(-1, None))
    return from_neighbours(
        *[
            jnp.concatenate([y_low[piece], row, y_high[piece]], axis=1)
            for row, piece in zip(rows, pieces)
        ],
        "gx",
    )


def edge_of(array):
    def edge(side, along_x):
        piece = slice(0, 1) if side == 0 else slice(-1, None)
        return array[piece] if along_x else array[:, piece]

    return edge


def from_group(value, axis, radix, stride):
    count = lax.axis_size(axis)
    return [
        lax.ppermute(value, axis, [(i, i ^ (k * stride)) for i in range(count)])
        for k in range(1, radix)
    ]


def to_members(blocks, differences):
    count = lax.axis_size("gy")
    return {
        k: lax.ppermute(blocks[k], "gy", [(i, i ^ k) for i in range(count)]) for k in differences
    }


def on_device(features, active_mask, owners, weight, channel_bias, cotangent):
    rows, across, channels, column = features.shape
    members_x, members = lax.axis_size("gx"), lax.axis_size("gy")
    at_x, me = lax.axis_index("gx"), lax.axis_index("gy")
    capacity = cotangent.shape[1] // members
    slot_count = members * capacity
    brick = cotangent.shape[3]
    vmem = pl.BlockSpec(memory_space=pltpu.VMEM)
    smem = pl.BlockSpec(memory_space=pltpu.SMEM)
    anywhere = pl.BlockSpec(memory_space=pltpu.HBM)
    conv_flops = 2 * rows * across * column * 27 * channels * channels
    scene_bytes = rows * across * column * channels
    far = [list(range(members // 2, members))[i::4] for i in range(4)]
    near = list(range(1, members // 2))
    message = (capacity, channels, brick)
    packed = jax.ShapeDtypeStruct(message, jnp.bfloat16)

    def masked(scene):
        def edge(side, along_x):
            mask = edge_of(active_mask)(side, along_x).astype(jnp.bfloat16)
            return edge_of(scene)(side, along_x) * mask[:, :, None, :]

        return edge

    columns = [masked(features)(side, False) for side in (0, -1)]
    halo = from_neighbours(*columns, "gy")
    rows_beside = [masked(features)(side, True) for side in (0, -1)]
    (owned,) = after([cotangent], *halo)
    returned = lax.all_to_all(
        owned.reshape(members, capacity * channels, brick),
        "gy",
        split_axis=0,
        concat_axis=0,
        tiled=True,
    ).reshape(slot_count, channels, brick)
    halo = (*halo, *halo_rows(rows_beside, *halo))

    me_list = me.reshape(1).astype(jnp.int32)
    owner_list = owners.reshape(-1)
    table = [pltpu.SMEM((owner_list.size,), jnp.int32), pltpu.SMEM((members,), jnp.int32)]
    slots = pltpu.VMEM((slot_count, channels, brick), jnp.bfloat16)
    sems = pltpu.SemaphoreType.DMA((members,))
    padded_shape = (rows + 2, across + 2, channels, column)
    kernel_shape = (3 * channels, 9 * channels)
    *outgoing, padded, factor, backward_kernel = call(
        functools.partial(forward_body, members),
        (
            *[packed] * members,
            jax.ShapeDtypeStruct(padded_shape, jnp.bfloat16),
            jax.ShapeDtypeStruct(features.shape, jnp.float32),
            jax.ShapeDtypeStruct(kernel_shape, jnp.bfloat16),
        ),
        [smem] * 2 + [vmem] * 8,
        [anywhere] * members + [vmem] * 3,
        [
            slots,
            pltpu.VMEM((rows * across, channels, column), jnp.bfloat16),
            pltpu.VMEM(kernel_shape, jnp.bfloat16),
            *table,
            sems,
        ],
        (
            me_list,
            owner_list,
            features,
            active_mask,
            *halo,
            weight.reshape(9, channels, 3 * channels),
            channel_bias.reshape(channels, 1),
        ),
        conv_flops,
        14 * scene_bytes,
        2 * scene_bytes,
    )
    arrived = {0: outgoing[0]}

    def send(differences, *others):
        messages = after([outgoing[k] for k in differences], *others)
        arrived.update(to_members(dict(zip(differences, messages)), differences))

    arrived.update(to_members(outgoing, near))
    (returned,) = after([returned], *[arrived[k] for k in near])
    slope = call(
        functools.partial(slope_body, capacity),
        jax.ShapeDtypeStruct(features.shape, jnp.bfloat16),
        [smem] * 2 + [vmem] * 2,
        vmem,
        [*table],
        (jnp.zeros((1,), jnp.int32), owner_list, returned, factor),
        0,
        0,
    )

    def in_turn(value, index):
        return after([value], *[arrived[k] for k in far[index]])[0]

    send(far[0], returned)
    send(far[1], returned)
    shares = call(
        kernel_grad_body,
        jax.ShapeDtypeStruct((members_x, 3, channels // members_x, 9 * channels), jnp.float32),
        [vmem] * 2,
        vmem,
        [pltpu.VMEM(kernel_shape, jnp.float32)],
        (slope, padded),
        0,
        0,
    )
    send(far[2], shares)
    shares = in_turn(shares, 0)
    total = lax.dynamic_index_in_dim(shares, at_x, 0, keepdims=False)
    for k in range(1, members_x):
        wanted = lax.dynamic_index_in_dim(shares, at_x ^ k, 0, keepdims=False)
        total = total + lax.ppermute(
            wanted.astype(jnp.bfloat16), "gx", [(i, i ^ k) for i in range(members_x)]
        ).astype(jnp.float32)
    columns = [edge_of(slope)(side, False) for side in (0, -1)]
    slope_halo = from_neighbours(*after(columns, total), "gy")
    for index, (radix, stride) in enumerate(((members // 4, 1), (4, members // 4))):
        total = in_turn(total, index + 1)
        sent = total.astype(jnp.bfloat16)
        terms = [
            term.astype(jnp.float32) for term in [sent, *from_group(sent, "gy", radix, stride)]
        ]
        while len(terms) > 1:
            terms = [terms[i] + terms[i + 1] for i in range(0, len(terms), 2)]
        total = terms[0]
        if index == 0:
            send(far[3], total)
    mine = total.astype(jnp.bfloat16)
    at_shares = jnp.stack([at_x ^ k for k in range(members_x)]).astype(jnp.int32)
    pieces = [mine, *from_group(mine, "gx", members_x, 1)]
    pieces = after(pieces, *[arrived[k] for k in far[3]])
    voxel_total = rows * across * column * members_x * members
    grad_weight = call(
        functools.partial(finish_body, voxel_total ** (-0.5)),
        jax.ShapeDtypeStruct((9, channels, 3 * channels), jnp.float32),
        [smem] + [vmem] * members_x,
        vmem,
        [pltpu.VMEM(shares.shape, jnp.float32)],
        (at_shares, *pieces),
        weight.size,
        6 * weight.size,
    ).reshape(weight.shape)
    rows_beside = [edge_of(slope)(side, True) for side in (0, -1)]
    slope_halo = (*slope_halo, *halo_rows(rows_beside, *slope_halo))
    grad_features = call(
        features_grad_body,
        jax.ShapeDtypeStruct(features.shape, jnp.bfloat16),
        [vmem] * 7,
        vmem,
        [pltpu.VMEM(padded_shape, jnp.bfloat16)],
        (slope, active_mask, *slope_halo, backward_kernel),
        conv_flops,
        5 * scene_bytes,
    )
    activations = jnp.zeros((members, *message), jnp.bfloat16)
    for k in [0, *near, *far[0], *far[1], *far[2], *far[3]]:
        activations = lax.dynamic_update_index_in_dim(activations, arrived[k], me ^ k, 0)
    activations = activations.reshape(1, slot_count, channels, brick)
    return activations, grad_features, grad_weight


def solution(mesh):
    in_specs = (
        P("gx", "gy", None, None),
        P("gx", "gy", None),
        P("gx", "gy", None),
        P(),
        P(),
        P("gx", "gy", None, None),
    )
    out_specs = (P("gx", "gy", None, None), P("gx", "gy", None, None), P())
    return jax.shard_map(
        on_device, mesh=mesh, in_specs=in_specs, out_specs=out_specs, check_vma=False
    )
```

time: 391 us -> 191 us (0.49); the launches traced: 384 us -> 190 us
  waiting for transfers between devices: 146 us -> 55.2 us
  matrix products: 89.2 us -> 0 us
  Pallas kernels: 0 us -> 40.1 us
  local copies, waits for them, and re-layouts: 56.4 us -> 22.9 us
  other arithmetic: 28.9 us -> 4.64 us
  starting transfers between devices: 49 us -> 65.9 us
  between operations: 14.6 us -> 0.98 us
    psum x1 -> x0, waiting for transfers between devices: 100 us -> none  [on_device(): grad_weight = lax.psum(tap_sums, ('gx', 'gy')) * voxel_total ** (-0.5)]
    dot_general x29 -> x0, matrix products: 89.2 us -> none  [the longest x18 68.1 us: conv_taps(): jnp.einsum('oc,xycz->xyoz', kernel[shift_x, shift_y], stacked[shift_x:shi...]
    pallas_call x0 -> x5, Pallas kernels: none -> 40.1 us  [call(): pl.pallas_call(body, out_shape=outs, in_specs=specs, out_specs=out_specs,...]
    ppermute x8 -> x25, starting transfers between devices: 38.6 us -> 61 us  [the longest x7 15.1 us: from_group(): lax.ppermute(value, axis, [(i, i ^ k * stride) for i in range(count)])]
    reshape x5 -> x1, local copies, waits for them, and re-layouts: 20.8 us -> 0.72 us  [on_device(): channel_bias.reshape(channels, 1)]
    concatenate x4, other arithmetic: 20.1 us -> 1.52 us  [halo_rows(): jnp.concatenate([y_low[piece], row, y_high[piece]], axis=1)]
    convert_element_type x4 -> x1, local copies, waits for them, and re-layouts: 16.4 us -> 0.05 us  [on_device(): wanted.astype(jnp.bfloat16)]
    unnamed x27 -> x49, local copies, waits for them, and re-layouts: 1.19 us -> 12.1 us
  transfers between devices with their start and end apart: 11 -> 26, of which waited for: 2 -> 11; matrix products, arithmetic and copies ran while one was open for 29% -> 7% of each run, Pallas kernels for 0% -> 20%
where the time goes in v1:
time: 191 us; the launch traced here: 190 us
  starting transfers between devices  65.9 us (35%)
  waiting for transfers between devices  55.2 us (29%)
  Pallas kernels  40.1 us (21%)
  local copies, waits for them, and re-layouts  22.9 us (12%)
  other arithmetic  4.64 us (2%)
    pallas_call x5, Pallas kernels, call(): pl.pallas_call(body, out_shape=outs, in_specs=specs, out_specs=out_specs,...  40.1 us
    ppermute x7, waiting for transfers between devices, to_members(): lax.ppermute(blocks[k], 'gy', [(i, i ^ k) for i in range(count)])  34.2 us
    ppermute x7, starting transfers between devices, from_group(): lax.ppermute(value, axis, [(i, i ^ k * stride) for i in range(count)])  15.1 us
    ppermute x4, starting transfers between devices, from_neighbours(): lax.ppermute(low_edge, axis, backward)  14 us
    ppermute x3, starting transfers between devices, on_device(): lax.ppermute(wanted.astype(jnp.bfloat16), 'gx', [(i, i ^ k) for i in rang...  12.7 us
    unnamed x49, local copies, waits for them, and re-layouts  12.1 us
    ppermute x7, starting transfers between devices, to_members(): lax.ppermute(blocks[k], 'gy', [(i, i ^ k) for i in range(count)])  10.1 us
    ppermute x4, waiting for transfers between devices, from_neighbours(): lax.ppermute(low_edge, axis, backward)  9.69 us
  transfers between devices with their start and end apart: 26, of which 11 were waited for; matrix products, arithmetic and copies ran while one was open for 7% of the time, Pallas kernels for 20%

profile of v1, /device:TPU:11, one launch (start us, length us, event | category | flops | bytes accessed | tf_op | source)
XLA Modules:
  0.0 189.8 jit_solution(4586204445784918140)
XLA Ops:
  2.0 1.1 slice_multiply_fusion.2
  3.1 3.1 %collective-permute-start = (bf16[8,1,96,128]{3,2,1,0:T(8,128)(2,1)S(1)}, bf16[8,1,96,128]{3,2,1,0:T(8,128)(2,1)S(1)}, u32[]{:S(2)}, u32[]{:S(2)}) collective-permute-start(bf16[8,1,96,128]{3,2,1,0:T(8,128)(2,1)S(1)} %get-tuple-element.62), channel_id=1, source_target_pairs={{0,1},{1,2},{2,3},{3,4},{4,5},{5,6},{6,7},{8,9},{9,10},{10,11},{11... | collective-permute-start | bytes 589832 | tf_op jit(solution)/shard_map/ppermute | solution.py:300
  6.2 3.0 %collective-permute-start.1 = (bf16[8,1,96,128]{3,2,1,0:T(8,128)(2,1)S(1)}, bf16[8,1,96,128]{3,2,1,0:T(8,128)(2,1)S(1)}, u32[]{:S(2)}, u32[]{:S(2)}) collective-permute-start(bf16[8,1,96,128]{3,2,1,0:T(8,128)(2,1)S(1)} %get-tuple-element.61), channel_id=1, source_target_pairs={{1,0},{2,1},{3,2},{4,3},{5,4},{6,5},{7,6},{9,8},{10,9},{11,10},{12... | collective-permute-start | bytes 589832 | tf_op jit(solution)/shard_map/ppermute | solution.py:300
  9.3 2.4 %collective-permute-done.y_low = bf16[8,1,96,128]{3,2,1,0:T(8,128)(2,1)S(1)} collective-permute-done((bf16[8,1,96,128]{3,2,1,0:T(8,128)(2,1)S(1)}, bf16[8,1,96,128]{3,2,1,0:T(8,128)(2,1)S(1)}, u32[]{:S(2)}, u32[]{:S(2)}) %collective-permute-start) | collective-permute-done | bytes 196640 | tf_op jit(solution)/shard_map/ppermute | solution.py:300
  11.6 5.3 %collective-permute-done.1.y_high = bf16[8,1,96,128]{3,2,1,0:T(8,128)(2,1)S(1)} collective-permute-done((bf16[8,1,96,128]{3,2,1,0:T(8,128)(2,1)S(1)}, bf16[8,1,96,128]{3,2,1,0:T(8,128)(2,1)S(1)}, u32[]{:S(2)}, u32[]{:S(2)}) %collective-permute-start.1) | collective-permute-done | bytes 196640 | tf_op jit(solution)/shard_map/ppermute | solution.py:300
  16.9 4.9 %all-to-all-start = ((bf16[8,384,512]{2,1,0:T(8,128)(2,1)}), bf16[8,384,512]{2,1,0:T(8,128)(2,1)S(1)}, u32[]{:S(2)}, u32[]{:S(2)}) async-start(bf16[8,384,512]{2,1,0:T(8,128)(2,1)} %bitcast.52), calls=%async_computation | async-start | bytes 6291456 | tf_op jit(solution)/shard_map/all_to_all | solution.py:365
  21.8 0.8 fusion.11
  22.6 1.1 slice_multiply_fusion
  24.4 1.3 collective-permute-start.2
  26.5 4.3 %collective-permute-start.3 = (bf16[1,10,96,128]{3,2,1,0:T(8,128)(2,1)}, bf16[1,10,96,128]{3,2,1,0:T(8,128)(2,1)}, u32[]{:S(2)}, u32[]{:S(2)}) collective-permute-start(bf16[1,10,96,128]{3,2,1,0:T(8,128)(2,1)} %pad_maximum_fusion.1), channel_id=1, source_target_pairs={{8,0},{16,8},{24,16},{9,1},{17,9},{25,17},{10,2},{18,10},{26,18},{... | collective-permute-start | bytes 737288 | tf_op jit(solution)/shard_map/ppermute | solution.py:300
  32.2 0.8 copy-done.1
  33.7 0.9 copy-done.5
  34.7 0.9 copy-done.7
  35.6 1.1 copy-done.9
  36.7 0.9 copy-done.19
  37.6 18.1 %shard_map.85 = (bf16[4,96,512]{2,1,0:T(8,128)(2,1)S(1)}, bf16[4,96,512]{2,1,0:T(8,128)(2,1)}, bf16[4,96,512]{2,1,0:T(8,128)(2,1)S(1)}, bf16[4,96,512]{2,1,0:T(8...) custom-call(s32[1]{0:T(128)} %bitcast.me_ref, ...), custom_call_target="tpu_custom_call" | custom-call | flops 4076863488 | bytes 11010048 | tf_op jit(solution)/shard_map/pallas_call | solution.py:279
  58.7 0.8 copy-done.16
  60.3 0.8 copy-done.20
  61.1 1.2 collective-permute-start.4
  62.6 1.2 collective-permute-start.6
  63.8 2.0 %broadcast_in_dim.32 = bf16[8,4,96,512]{3,2,1,0:T(8,128)(2,1)} broadcast(bf16[]{:T(256)} %constant.43.clone.1), dimensions={} | broadcast | bytes 3145730 | tf_op jit(solution)/shard_map/broadcast_in_dim | solution.py:493
  66.6 8.0 %collective-permute-done.4 = bf16[4,96,512]{2,1,0:T(8,128)(2,1)} collective-permute-done((bf16[4,96,512]{2,1,0:T(8,128)(2,1)}, bf16[4,96,512]{2,1,0:T(8,128)(2,1)}, u32[]{:S(2)}, u32[]{:S(2)}) %collective-permute-start.4) | collective-permute-done | bytes 393248 | tf_op jit(solution)/shard_map/ppermute | solution.py:333
  74.6 1.8 bitcast_dynamic-update-slice_fusion.6
  76.4 6.1 %collective-permute-done.5 = bf16[4,96,512]{2,1,0:T(8,128)(2,1)S(1)} collective-permute-done((bf16[4,96,512]{2,1,0:T(8,128)(2,1)}, bf16[4,96,512]{2,1,0:T(8,128)(2,1)S(1)}, u32[]{:S(2)}, u32[]{:S(2)}) %collective-permute-start.5) | collective-permute-done | bytes 393248 | tf_op jit(solution)/shard_map/ppermute | solution.py:333
  83.3 8.2 %collective-permute-done.6 = bf16[4,96,512]{2,1,0:T(8,128)(2,1)S(1)} collective-permute-done((bf16[4,96,512]{2,1,0:T(8,128)(2,1)}, bf16[4,96,512]{2,1,0:T(8,128)(2,1)S(1)}, u32[]{:S(2)}, u32[]{:S(2)}) %collective-permute-start.6) | collective-permute-done | bytes 393248 | tf_op jit(solution)/shard_map/ppermute | solution.py:333
  92.2 1.6 collective-permute-start.7
  93.8 4.1 %collective-permute-start.8 = (bf16[4,96,512]{2,1,0:T(8,128)(2,1)}, bf16[4,96,512]{2,1,0:T(8,128)(2,1)S(1)}, u32[]{:S(2)}, u32[]{:S(2)}) collective-permute-start(bf16[4,96,512]{2,1,0:T(8,128)(2,1)} %copy-done.14), channel_id=1, source_target_pairs={{0,5},{1,4},{2,7},{3,6},{4,1},{5,0},{6,3},{7,2},{8,13},{9,12},{10,... | collective-permute-start | bytes 1179656 | tf_op jit(solution)/shard_map/ppermute | solution.py:333
  97.9 4.7 %shard_map.86.slope_ref = bf16[8,8,96,128]{3,2,1,0:T(8,128)(2,1)S(1)} custom-call(s32[1]{0:T(128)} %constant.52.clone.1.zero_ref, s32[16]{0:T(128)S(1)} %bitcast.50, bf16[32,96,512]{2,1,0:T(8,128)(2,1)S(1)} %bitcast.48, f32[8,8,96,128]{3,2,1,0:T(8,128)} %get-tuple-element.40.factor_ref), custom_call_target="tpu_custom_call" | custom-call | tf_op jit(solution)/shard_map/pallas_call | solution.py:279
  102.6 6.8 %shard_map.87 = f32[4,3,24,864]{3,2,1,0:T(8,128)S(1)} custom-call(bf16[8,8,96,128]{3,2,1,0:T(8,128)(2,1)S(1)} %shard_map.86.slope_ref, bf16[10,10,96,128]{3,2,1,0:T(8,128)(2,1)S(1)} %copy-done), custom_call_target="tpu_custom_call" | custom-call | tf_op jit(solution)/shard_map/pallas_call | solution.py:279
  109.7 11.8 %collective-permute-done.7 = bf16[4,96,512]{2,1,0:T(8,128)(2,1)S(1)} collective-permute-done((bf16[4,96,512]{2,1,0:T(8,128)(2,1)}, bf16[4,96,512]{2,1,0:T(8,128)(2,1)S(1)}, u32[]{:S(2)}, u32[]{:S(2)}) %collective-permute-start.7) | collective-permute-done | bytes 393248 | tf_op jit(solution)/shard_map/ppermute | solution.py:333
  121.6 10.0 %collective-permute-start.10 = (bf16[3,24,864]{2,1,0:T(8,128)(2,1)S(1)}, bf16[3,24,864]{2,1,0:T(8,128)(2,1)S(1)}, u32[]{:S(2)}, u32[]{:S(2)}) collective-permute-start(bf16[3,24,864]{2,1,0:T(8,128)(2,1)S(1)} %get-tuple-element.63), channel_id=1, source_target_pairs={{0,8},{8,0},{16,24},{24,16},{1,9},{9,1},{17,25},{25,17},{2,10},{10... | collective-permute-start | bytes 373256 | tf_op jit(solution)/shard_map/ppermute | solution.py:450
  131.6 2.3 %collective-permute-start.11 = (bf16[3,24,864]{2,1,0:T(8,128)(2,1)S(1)}, bf16[3,24,864]{2,1,0:T(8,128)(2,1)S(1)}, u32[]{:S(2)}, u32[]{:S(2)}) collective-permute-start(bf16[3,24,864]{2,1,0:T(8,128)(2,1)S(1)} %get-tuple-element.65), channel_id=1, source_target_pairs={{0,16},{8,24},{16,0},{24,8},{1,17},{9,25},{17,1},{25,9},{2,18},{10... | collective-permute-start | bytes 373256 | tf_op jit(solution)/shard_map/ppermute | solution.py:450
  135.0 2.3 %collective-permute-done.11 = bf16[3,24,864]{2,1,0:T(8,128)(2,1)S(1)} collective-permute-done((bf16[3,24,864]{2,1,0:T(8,128)(2,1)S(1)}, bf16[3,24,864]{2,1,0:T(8,128)(2,1)S(1)}, u32[]{:S(2)}, u32[]{:S(2)}) %collective-permute-start.11) | collective-permute-done | bytes 124448 | tf_op jit(solution)/shard_map/ppermute | solution.py:450
  137.4 3.3 %collective-permute-done.12 = bf16[3,24,864]{2,1,0:T(8,128)(2,1)S(1)} collective-permute-done((bf16[3,24,864]{2,1,0:T(8,128)(2,1)S(1)}, bf16[3,24,864]{2,1,0:T(8,128)(2,1)S(1)}, u32[]{:S(2)}, u32[]{:S(2)}) %collective-permute-start.12) | collective-permute-done | bytes 124448 | tf_op jit(solution)/shard_map/ppermute | solution.py:450
  140.9 0.8 bitcast_dynamic-update-slice_fusion.2
  141.6 3.3 %collective-permute-start.15 = (bf16[8,1,96,128]{3,2,1,0:T(8,128)(2,1)S(1)}, bf16[8,1,96,128]{3,2,1,0:T(8,128)(2,1)S(1)}, u32[]{:S(2)}, u32[]{:S(2)}) collective-permute-start(bf16[8,1,96,128]{3,2,1,0:T(8,128)(2,1)S(1)} %get-tuple-element.47), channel_id=1, source_target_pairs={{0,1},{1,2},{2,3},{3,4},{4,5},{5,6},{6,7},{8,9},{9,10},{10,11},{11... | collective-permute-start | bytes 589832 | tf_op jit(solution)/shard_map/ppermute | solution.py:300
  145.0 4.3 %collective-permute-start.16 = (bf16[8,1,96,128]{3,2,1,0:T(8,128)(2,1)S(1)}, bf16[8,1,96,128]{3,2,1,0:T(8,128)(2,1)S(1)}, u32[]{:S(2)}, u32[]{:S(2)}) collective-permute-start(bf16[8,1,96,128]{3,2,1,0:T(8,128)(2,1)S(1)} %get-tuple-element.48), channel_id=1, source_target_pairs={{1,0},{2,1},{3,2},{4,3},{5,4},{6,5},{7,6},{9,8},{10,9},{11,10},{12... | collective-permute-start | bytes 589832 | tf_op jit(solution)/shard_map/ppermute | solution.py:300
  149.5 2.3 %collective-permute-start.20 = (bf16[3,24,864]{2,1,0:T(8,128)(2,1)S(1)}, bf16[3,24,864]{2,1,0:T(8,128)(2,1)S(1)}, u32[]{:S(2)}, u32[]{:S(2)}) collective-permute-start(bf16[3,24,864]{2,1,0:T(8,128)(2,1)S(1)} %convert_add_fusion), channel_id=1, source_target_pairs={{0,4},{1,5},{2,6},{3,7},{4,0},{5,1},{6,2},{7,3},{8,12},{9,13},{10,... | collective-permute-start | bytes 373256 | tf_op jit(solution)/shard_map/ppermute | solution.py:325
  152.6 4.4 %collective-permute-done.16.y_high = bf16[8,1,96,128]{3,2,1,0:T(8,128)(2,1)S(1)} collective-permute-done((bf16[8,1,96,128]{3,2,1,0:T(8,128)(2,1)S(1)}, bf16[8,1,96,128]{3,2,1,0:T(8,128)(2,1)S(1)}, u32[]{:S(2)}, u32[]{:S(2)}) %collective-permute-start.16) | collective-permute-done | bytes 196640 | tf_op jit(solution)/shard_map/ppermute | solution.py:300
  157.0 2.4 %collective-permute-start.18 = (bf16[1,10,96,128]{3,2,1,0:T(8,128)(2,1)S(1)}, bf16[1,10,96,128]{3,2,1,0:T(8,128)(2,1)S(1)}, u32[]{:S(2)}, u32[]{:S(2)}) collective-permute-start(bf16[1,10,96,128]{3,2,1,0:T(8,128)(2,1)S(1)} %pad_maximum_fusion.3), channel_id=1, source_target_pairs={{8,0},{16,8},{24,16},{9,1},{17,9},{25,17},{10,2},{18,10},{26,18},{... | collective-permute-start | bytes 737288 | tf_op jit(solution)/shard_map/ppermute | solution.py:300
  159.5 1.3 collective-permute-start.17
  160.8 0.8 bitcast_dynamic-update-slice_fusion.1
  161.5 1.7 collective-permute-start.14
  163.2 2.8 %collective-permute-done.21 = bf16[3,24,864]{2,1,0:T(8,128)(2,1)S(1)} collective-permute-done((bf16[3,24,864]{2,1,0:T(8,128)(2,1)S(1)}, bf16[3,24,864]{2,1,0:T(8,128)(2,1)S(1)}, u32[]{:S(2)}, u32[]{:S(2)}) %collective-permute-start.21) | collective-permute-done | bytes 124448 | tf_op jit(solution)/shard_map/ppermute | solution.py:325
  166.1 10.6 %collective-permute-start.22 = (bf16[3,24,864]{2,1,0:T(8,128)(2,1)S(1)}, bf16[3,24,864]{2,1,0:T(8,128)(2,1)S(1)}, u32[]{:S(2)}, u32[]{:S(2)}) collective-permute-start(bf16[3,24,864]{2,1,0:T(8,128)(2,1)S(1)} %add_convert_fusion.refs_0_), channel_id=1, source_target_pairs={{0,8},{8,0},{16,24},{24,16},{1,9},{9,1},{17,25},{25,17},{2,10},{10... | collective-permute-start | bytes 373256 | tf_op jit(solution)/shard_map/ppermute | solution.py:325
  176.8 1.7 collective-permute-start.24
  178.5 8.4 %shard_map.88 = bf16[8,8,96,128]{3,2,1,0:T(8,128)(2,1)} custom-call(bf16[8,8,96,128]{3,2,1,0:T(8,128)(2,1)S(1)} %shard_map.86.slope_ref, s32[8,8,128]{2,1,0:T(8,128)S(1)} %copy-done.3, bf16[8,1,96,128]{3,2,1,0:T(8,128)(2,1)S(1)} %collective-permute-done.15.y_low, bf16[8,1,96,128]{3,2,1,0:T(8,128)(2,1)S(1)} %collective-permute-done.16.y_high, ...), custom_call_target="tpu_custom_call" | custom-call | flops 4076863488 | bytes 3932160 | tf_op jit(solution)/shard_map/pallas_call | solution.py:279
  186.9 2.1 %shard_map.89 = f32[9,96,288]{2,1,0:T(8,128)} custom-call(s32[4]{0:T(128)S(1)} %pad_add_fusion.at_ref, bf16[3,24,864]{2,1,0:T(8,128)(2,1)S(1)} %add_convert_fusion.refs_0_, bf16[3,24,864]{2,1,0:T(8,128)(2,1)S(1)} %collective-permute-done.22.refs_1_, bf16[3,24,864]{2,1,0:T(8,128)(2,1)S(1)} %collective-permute-done.23.refs_2_, ...), custom_call_target="tpu_custom_call" | custom-call | flops 248832 | bytes 1492992 | tf_op jit(solution)/shard_map/pallas_call | solution.py:279
  (88 shorter events, 14.8 us)
Async XLA Ops:
  3.1 8.6 %collective-permute-start = (bf16[8,1,96,128]{3,2,1,0:T(8,128)(2,1)S(1)}, bf16[8,1,96,128]{3,2,1,0:T(8,128)(2,1)S(1)}, u32[]{:S(2)}, u32[]{:S(2)}) collective-permute-start(bf16[8,1,96,128]{3,2,1,0:T(8,128)(2,1)S(1)} %get-tuple-element.62), channel_id=1, source_target_pairs={{0,1},{1,2},{2,3},{3,4},{4,5},{5,6},{6,7},{8,9},{9,10},{10,11},{11... | collective-permute-start | bytes 589832 | tf_op jit(solution)/shard_map/ppermute | solution.py:300
  6.2 10.7 %collective-permute-start.1 = (bf16[8,1,96,128]{3,2,1,0:T(8,128)(2,1)S(1)}, bf16[8,1,96,128]{3,2,1,0:T(8,128)(2,1)S(1)}, u32[]{:S(2)}, u32[]{:S(2)}) collective-permute-start(bf16[8,1,96,128]{3,2,1,0:T(8,128)(2,1)S(1)} %get-tuple-element.61), channel_id=1, source_target_pairs={{1,0},{2,1},{3,2},{4,3},{5,4},{6,5},{7,6},{9,8},{10,9},{11,10},{12... | collective-permute-start | bytes 589832 | tf_op jit(solution)/shard_map/ppermute | solution.py:300
  11.6 12.0 %copy-start.4 = (bf16[8,1,96,128]{3,2,1,0:T(8,128)(2,1)}, bf16[8,1,96,128]{3,2,1,0:T(8,128)(2,1)S(1)}, u32[]{:S(2)}) copy-start(bf16[8,1,96,128]{3,2,1,0:T(8,128)(2,1)S(1)} %collective-permute-done.y_low) | copy-start | bytes 589828
  16.9 6.8 %copy-start.6 = (bf16[8,1,96,128]{3,2,1,0:T(8,128)(2,1)}, bf16[8,1,96,128]{3,2,1,0:T(8,128)(2,1)S(1)}, u32[]{:S(2)}) copy-start(bf16[8,1,96,128]{3,2,1,0:T(8,128)(2,1)S(1)} %collective-permute-done.1.y_high) | copy-start | bytes 589828
  16.9 13.9 %copy-start.23 = (f32[96]{0:T(128)S(1)}, f32[96]{0:T(128)}, u32[]{:S(2)}) copy-start(f32[96]{0:T(128)} %param.10) | copy-start | bytes 1156
  16.9 15.3 %copy-start.8 = (s32[1,1,16]{2,1,0:T(1,128)S(1)}, s32[1,1,16]{2,1,0:T(1,128)}, u32[]{:S(2)}) copy-start(s32[1,1,16]{2,1,0:T(1,128)} %param.8) | copy-start | bytes 196
  16.9 75.3 %all-to-all-start = ((bf16[8,384,512]{2,1,0:T(8,128)(2,1)}), bf16[8,384,512]{2,1,0:T(8,128)(2,1)S(1)}, u32[]{:S(2)}, u32[]{:S(2)}) async-start(bf16[8,384,512]{2,1,0:T(8,128)(2,1)} %bitcast.52), calls=%async_computation | async-start | bytes 6291456 | tf_op jit(solution)/shard_map/all_to_all | solution.py:365
  24.4 7.0 %collective-permute-start.2 = (bf16[1,10,96,128]{3,2,1,0:T(8,128)(2,1)}, bf16[1,10,96,128]{3,2,1,0:T(8,128)(2,1)S(1)}, u32[]{:S(2)}, u32[]{:S(2)}) collective-permute-start(bf16[1,10,96,128]{3,2,1,0:T(8,128)(2,1)} %pad_maximum_fusion), channel_id=1, source_target_pairs={{0,8},{8,16},{16,24},{1,9},{9,17},{17,25},{2,10},{10,18},{18,26},{... | collective-permute-start | bytes 737288 | tf_op jit(solution)/shard_map/ppermute | solution.py:300
  26.5 5.7 %collective-permute-start.3 = (bf16[1,10,96,128]{3,2,1,0:T(8,128)(2,1)}, bf16[1,10,96,128]{3,2,1,0:T(8,128)(2,1)}, u32[]{:S(2)}, u32[]{:S(2)}) collective-permute-start(bf16[1,10,96,128]{3,2,1,0:T(8,128)(2,1)} %pad_maximum_fusion.1), channel_id=1, source_target_pairs={{8,0},{16,8},{24,16},{9,1},{17,9},{25,17},{10,2},{18,10},{26,18},{... | collective-permute-start | bytes 737288 | tf_op jit(solution)/shard_map/ppermute | solution.py:300
  32.2 0.8 copy-start.1
  33.0 0.8 copy-start.2
  33.7 0.9 copy-start.5
  34.7 0.9 copy-start.7
  35.6 1.1 copy-start.9
  36.7 0.9 copy-start.19
  55.7 0.7 copy-start.10
  56.5 0.7 copy-start.12
  57.2 0.8 copy-start.14
  58.0 0.8 copy-start.15
  58.7 0.8 copy-start.16
  59.5 0.8 copy-start.17
  60.3 0.8 copy-start.20
  61.1 13.6 %collective-permute-start.4 = (bf16[4,96,512]{2,1,0:T(8,128)(2,1)}, bf16[4,96,512]{2,1,0:T(8,128)(2,1)}, u32[]{:S(2)}, u32[]{:S(2)}) collective-permute-start(bf16[4,96,512]{2,1,0:T(8,128)(2,1)} %get-tuple-element.30), channel_id=1, source_target_pairs={{0,1},{1,0},{2,3},{3,2},{4,5},{5,4},{6,7},{7,6},{8,9},{9,8},{10,11... | collective-permute-start | bytes 1179656 | tf_op jit(solution)/shard_map/ppermute | solution.py:333
  62.3 20.2 %collective-permute-start.5 = (bf16[4,96,512]{2,1,0:T(8,128)(2,1)}, bf16[4,96,512]{2,1,0:T(8,128)(2,1)S(1)}, u32[]{:S(2)}, u32[]{:S(2)}) collective-permute-start(bf16[4,96,512]{2,1,0:T(8,128)(2,1)} %copy-done.17), channel_id=1, source_target_pairs={{0,2},{1,3},{2,0},{3,1},{4,6},{5,7},{6,4},{7,5},{8,10},{9,11},{10,... | collective-permute-start | bytes 1179656 | tf_op jit(solution)/shard_map/ppermute | solution.py:333
  62.6 28.8 %collective-permute-start.6 = (bf16[4,96,512]{2,1,0:T(8,128)(2,1)}, bf16[4,96,512]{2,1,0:T(8,128)(2,1)S(1)}, u32[]{:S(2)}, u32[]{:S(2)}) collective-permute-start(bf16[4,96,512]{2,1,0:T(8,128)(2,1)} %copy-done.16), channel_id=1, source_target_pairs={{0,3},{1,2},{2,1},{3,0},{4,7},{5,6},{6,5},{7,4},{8,11},{9,10},{10,... | collective-permute-start | bytes 1179656 | tf_op jit(solution)/shard_map/ppermute | solution.py:333
  92.2 29.3 %collective-permute-start.7 = (bf16[4,96,512]{2,1,0:T(8,128)(2,1)}, bf16[4,96,512]{2,1,0:T(8,128)(2,1)S(1)}, u32[]{:S(2)}, u32[]{:S(2)}) collective-permute-start(bf16[4,96,512]{2,1,0:T(8,128)(2,1)} %copy-done.15), channel_id=1, source_target_pairs={{0,4},{1,5},{2,6},{3,7},{4,0},{5,1},{6,2},{7,3},{8,12},{9,13},{10,... | collective-permute-start | bytes 1179656 | tf_op jit(solution)/shard_map/ppermute | solution.py:333
  93.8 46.9 %collective-permute-start.8 = (bf16[4,96,512]{2,1,0:T(8,128)(2,1)}, bf16[4,96,512]{2,1,0:T(8,128)(2,1)S(1)}, u32[]{:S(2)}, u32[]{:S(2)}) collective-permute-start(bf16[4,96,512]{2,1,0:T(8,128)(2,1)} %copy-done.14), channel_id=1, source_target_pairs={{0,5},{1,4},{2,7},{3,6},{4,1},{5,0},{6,3},{7,2},{8,13},{9,12},{10,... | collective-permute-start | bytes 1179656 | tf_op jit(solution)/shard_map/ppermute | solution.py:333
  97.9 4.7 %copy-start = (bf16[10,10,96,128]{3,2,1,0:T(8,128)(2,1)S(1)}, bf16[10,10,96,128]{3,2,1,0:T(8,128)(2,1)}, u32[]{:S(2)}) copy-start(bf16[10,10,96,128]{3,2,1,0:T(8,128)(2,1)} %get-tuple-element.41.padded_ref) | copy-start | bytes 7372804
  102.6 6.9 %copy-start.13 = (bf16[4,96,512]{2,1,0:T(8,128)(2,1)S(1)}, bf16[4,96,512]{2,1,0:T(8,128)(2,1)}, u32[]{:S(2)}) copy-start(bf16[4,96,512]{2,1,0:T(8,128)(2,1)} %copy-done.12) | copy-start | bytes 1179652
  109.5 39.9 %collective-permute-start.9 = (bf16[4,96,512]{2,1,0:T(8,128)(2,1)S(1)}, bf16[4,96,512]{2,1,0:T(8,128)(2,1)S(1)}, u32[]{:S(2)}, u32[]{:S(2)}) collective-permute-start(bf16[4,96,512]{2,1,0:T(8,128)(2,1)S(1)} %copy-done.13), channel_id=1, source_target_pairs={{0,6},{1,7},{2,4},{3,5},{4,2},{5,3},{6,0},{7,1},{8,14},{9,15},{10,... | collective-permute-start | bytes 1179656 | tf_op jit(solution)/shard_map/ppermute | solution.py:333
  109.6 52.0 %copy-start.11 = (bf16[4,96,512]{2,1,0:T(8,128)(2,1)S(1)}, bf16[4,96,512]{2,1,0:T(8,128)(2,1)}, u32[]{:S(2)}) copy-start(bf16[4,96,512]{2,1,0:T(8,128)(2,1)} %copy-done.10) | copy-start | bytes 1179652
  109.6 68.8 %copy-start.3 = (s32[8,8,128]{2,1,0:T(8,128)S(1)}, s32[8,8,128]{2,1,0:T(8,128)}, u32[]{:S(2)}) copy-start(s32[8,8,128]{2,1,0:T(8,128)} %mask_ref.3) | copy-start | bytes 98308
  109.6 68.8 %copy-start.21 = (bf16[288,864]{1,0:T(8,128)(2,1)S(1)}, bf16[288,864]{1,0:T(8,128)(2,1)}, u32[]{:S(2)}) copy-start(bf16[288,864]{1,0:T(8,128)(2,1)} %copy-done.20) | copy-start | bytes 1492996
  121.6 13.5 %collective-permute-start.10 = (bf16[3,24,864]{2,1,0:T(8,128)(2,1)S(1)}, bf16[3,24,864]{2,1,0:T(8,128)(2,1)S(1)}, u32[]{:S(2)}, u32[]{:S(2)}) collective-permute-start(bf16[3,24,864]{2,1,0:T(8,128)(2,1)S(1)} %get-tuple-element.63), channel_id=1, source_target_pairs={{0,8},{8,0},{16,24},{24,16},{1,9},{9,1},{17,25},{25,17},{2,10},{10... | collective-permute-start | bytes 373256 | tf_op jit(solution)/shard_map/ppermute | solution.py:450
  131.6 5.8 %collective-permute-start.11 = (bf16[3,24,864]{2,1,0:T(8,128)(2,1)S(1)}, bf16[3,24,864]{2,1,0:T(8,128)(2,1)S(1)}, u32[]{:S(2)}, u32[]{:S(2)}) collective-permute-start(bf16[3,24,864]{2,1,0:T(8,128)(2,1)S(1)} %get-tuple-element.65), channel_id=1, source_target_pairs={{0,16},{8,24},{16,0},{24,8},{1,17},{9,25},{17,1},{25,9},{2,18},{10... | collective-permute-start | bytes 373256 | tf_op jit(solution)/shard_map/ppermute | solution.py:450
  133.9 6.8 %collective-permute-start.12 = (bf16[3,24,864]{2,1,0:T(8,128)(2,1)S(1)}, bf16[3,24,864]{2,1,0:T(8,128)(2,1)S(1)}, u32[]{:S(2)}, u32[]{:S(2)}) collective-permute-start(bf16[3,24,864]{2,1,0:T(8,128)(2,1)S(1)} %get-tuple-element.64), channel_id=1, source_target_pairs={{0,24},{8,16},{16,8},{24,0},{1,25},{9,17},{17,9},{25,1},{2,26},{10... | collective-permute-start | bytes 373256 | tf_op jit(solution)/shard_map/ppermute | solution.py:450
  140.8 8.6 %collective-permute-start.13 = (bf16[3,24,864]{2,1,0:T(8,128)(2,1)S(1)}, bf16[3,24,864]{2,1,0:T(8,128)(2,1)S(1)}, u32[]{:S(2)}, u32[]{:S(2)}) collective-permute-start(bf16[3,24,864]{2,1,0:T(8,128)(2,1)S(1)} %fusion.1), channel_id=1, source_target_pairs={{0,1},{1,0},{2,3},{3,2},{4,5},{5,4},{6,7},{7,6},{8,9},{9,8},{10,11... | collective-permute-start | bytes 373256 | tf_op jit(solution)/shard_map/ppermute | solution.py:325
  141.6 10.9 %collective-permute-start.15 = (bf16[8,1,96,128]{3,2,1,0:T(8,128)(2,1)S(1)}, bf16[8,1,96,128]{3,2,1,0:T(8,128)(2,1)S(1)}, u32[]{:S(2)}, u32[]{:S(2)}) collective-permute-start(bf16[8,1,96,128]{3,2,1,0:T(8,128)(2,1)S(1)} %get-tuple-element.47), channel_id=1, source_target_pairs={{0,1},{1,2},{2,3},{3,4},{4,5},{5,6},{6,7},{8,9},{9,10},{10,11},{11... | collective-permute-start | bytes 589832 | tf_op jit(solution)/shard_map/ppermute | solution.py:300
  145.0 12.0 %collective-permute-start.16 = (bf16[8,1,96,128]{3,2,1,0:T(8,128)(2,1)S(1)}, bf16[8,1,96,128]{3,2,1,0:T(8,128)(2,1)S(1)}, u32[]{:S(2)}, u32[]{:S(2)}) collective-permute-start(bf16[8,1,96,128]{3,2,1,0:T(8,128)(2,1)S(1)} %get-tuple-element.48), channel_id=1, source_target_pairs={{1,0},{2,1},{3,2},{4,3},{5,4},{6,5},{7,6},{9,8},{10,9},{11,10},{12... | collective-permute-start | bytes 589832 | tf_op jit(solution)/shard_map/ppermute | solution.py:300
  149.4 12.2 %collective-permute-start.19 = (bf16[3,24,864]{2,1,0:T(8,128)(2,1)S(1)}, bf16[3,24,864]{2,1,0:T(8,128)(2,1)S(1)}, u32[]{:S(2)}, u32[]{:S(2)}) collective-permute-start(bf16[3,24,864]{2,1,0:T(8,128)(2,1)S(1)} %convert_add_fusion), channel_id=1, source_target_pairs={{0,2},{1,3},{2,0},{3,1},{4,6},{5,7},{6,4},{7,5},{8,10},{9,11},{10,... | collective-permute-start | bytes 373256 | tf_op jit(solution)/shard_map/ppermute | solution.py:325
  149.5 13.8 %collective-permute-start.20 = (bf16[3,24,864]{2,1,0:T(8,128)(2,1)S(1)}, bf16[3,24,864]{2,1,0:T(8,128)(2,1)S(1)}, u32[]{:S(2)}, u32[]{:S(2)}) collective-permute-start(bf16[3,24,864]{2,1,0:T(8,128)(2,1)S(1)} %convert_add_fusion), channel_id=1, source_target_pairs={{0,4},{1,5},{2,6},{3,7},{4,0},{5,1},{6,2},{7,3},{8,12},{9,13},{10,... | collective-permute-start | bytes 373256 | tf_op jit(solution)/shard_map/ppermute | solution.py:325
  151.7 14.3 %collective-permute-start.21 = (bf16[3,24,864]{2,1,0:T(8,128)(2,1)S(1)}, bf16[3,24,864]{2,1,0:T(8,128)(2,1)S(1)}, u32[]{:S(2)}, u32[]{:S(2)}) collective-permute-start(bf16[3,24,864]{2,1,0:T(8,128)(2,1)S(1)} %convert_add_fusion), channel_id=1, source_target_pairs={{0,6},{1,7},{2,4},{3,5},{4,2},{5,3},{6,0},{7,1},{8,14},{9,15},{10,... | collective-permute-start | bytes 373256 | tf_op jit(solution)/shard_map/ppermute | solution.py:325
  157.0 19.7 %collective-permute-start.18 = (bf16[1,10,96,128]{3,2,1,0:T(8,128)(2,1)S(1)}, bf16[1,10,96,128]{3,2,1,0:T(8,128)(2,1)S(1)}, u32[]{:S(2)}, u32[]{:S(2)}) collective-permute-start(bf16[1,10,96,128]{3,2,1,0:T(8,128)(2,1)S(1)} %pad_maximum_fusion.3), channel_id=1, source_target_pairs={{8,0},{16,8},{24,16},{9,1},{17,9},{25,17},{10,2},{18,10},{26,18},{... | collective-permute-start | bytes 737288 | tf_op jit(solution)/shard_map/ppermute | solution.py:300
  159.5 19.0 %collective-permute-start.17 = (bf16[1,10,96,128]{3,2,1,0:T(8,128)(2,1)S(1)}, bf16[1,10,96,128]{3,2,1,0:T(8,128)(2,1)S(1)}, u32[]{:S(2)}, u32[]{:S(2)}) collective-permute-start(bf16[1,10,96,128]{3,2,1,0:T(8,128)(2,1)S(1)} %pad_maximum_fusion.2), channel_id=1, source_target_pairs={{0,8},{8,16},{16,24},{1,9},{9,17},{17,25},{2,10},{10,18},{18,26},{... | collective-permute-start | bytes 737288 | tf_op jit(solution)/shard_map/ppermute | solution.py:300
  161.5 25.3 %collective-permute-start.14 = (bf16[4,96,512]{2,1,0:T(8,128)(2,1)S(1)}, bf16[4,96,512]{2,1,0:T(8,128)(2,1)S(1)}, u32[]{:S(2)}, u32[]{:S(2)}) collective-permute-start(bf16[4,96,512]{2,1,0:T(8,128)(2,1)S(1)} %copy-done.11), channel_id=1, source_target_pairs={{0,7},{1,6},{2,5},{3,4},{4,3},{5,2},{6,1},{7,0},{8,15},{9,14},{10,... | collective-permute-start | bytes 1179656 | tf_op jit(solution)/shard_map/ppermute | solution.py:333
  166.1 20.7 %collective-permute-start.22 = (bf16[3,24,864]{2,1,0:T(8,128)(2,1)S(1)}, bf16[3,24,864]{2,1,0:T(8,128)(2,1)S(1)}, u32[]{:S(2)}, u32[]{:S(2)}) collective-permute-start(bf16[3,24,864]{2,1,0:T(8,128)(2,1)S(1)} %add_convert_fusion.refs_0_), channel_id=1, source_target_pairs={{0,8},{8,0},{16,24},{24,16},{1,9},{9,1},{17,25},{25,17},{2,10},{10... | collective-permute-start | bytes 373256 | tf_op jit(solution)/shard_map/ppermute | solution.py:325
  176.7 10.1 %collective-permute-start.23 = (bf16[3,24,864]{2,1,0:T(8,128)(2,1)S(1)}, bf16[3,24,864]{2,1,0:T(8,128)(2,1)S(1)}, u32[]{:S(2)}, u32[]{:S(2)}) collective-permute-start(bf16[3,24,864]{2,1,0:T(8,128)(2,1)S(1)} %add_convert_fusion.refs_0_), channel_id=1, source_target_pairs={{0,16},{8,24},{16,0},{24,8},{1,17},{9,25},{17,1},{25,9},{2,18},{10... | collective-permute-start | bytes 373256 | tf_op jit(solution)/shard_map/ppermute | solution.py:325
  176.8 10.1 %collective-permute-start.24 = (bf16[3,24,864]{2,1,0:T(8,128)(2,1)S(1)}, bf16[3,24,864]{2,1,0:T(8,128)(2,1)S(1)}, u32[]{:S(2)}, u32[]{:S(2)}) collective-permute-start(bf16[3,24,864]{2,1,0:T(8,128)(2,1)S(1)} %add_convert_fusion.refs_0_), channel_id=1, source_target_pairs={{0,24},{8,16},{16,8},{24,0},{1,25},{9,17},{17,9},{25,1},{2,26},{10... | collective-permute-start | bytes 373256 | tf_op jit(solution)/shard_map/ppermute | solution.py:325
  (2 other events, 1.3 us)

commit v2 on v1

--- a/solution.py
+++ b/solution.py
@@ -452,6 +452,7 @@
         ).astype(jnp.float32)
     columns = [edge_of(slope)(side, False) for side in (0, -1)]
     slope_halo = from_neighbours(*after(columns, total), "gy")
+    send(far[3], total)
     for index, (radix, stride) in enumerate(((members // 4, 1), (4, members // 4))):
         total = in_turn(total, index + 1)
         sent = total.astype(jnp.bfloat16)
@@ -461,8 +462,6 @@
         while len(terms) > 1:
             terms = [terms[i] + terms[i + 1] for i in range(0, len(terms), 2)]
         total = terms[0]
-        if index == 0:
-            send(far[3], total)
     mine = total.astype(jnp.bfloat16)
     at_shares = jnp.stack([at_x ^ k for k in range(members_x)]).astype(jnp.int32)
     pieces = [mine, *from_group(mine, "gx", members_x, 1)]
@@ -487,8 +486,8 @@
         vmem,
         [pltpu.VMEM(padded_shape, jnp.bfloat16)],
         (slope, active_mask, *slope_halo, backward_kernel),
-        conv_flops,
-        5 * scene_bytes,
+        0,
+        0,
     )
     activations = jnp.zeros((members, *message), jnp.bfloat16)
     for k in [0, *near, *far[0], *far[1], *far[2], *far[3]]:

time: 191 us -> 210 us (1.099)
  starting transfers between devices: 65.9 us -> 76 us
  waiting for transfers between devices: 55.2 us -> 62.8 us
    ppermute x7, starting transfers between devices: 15.1 us -> 26.4 us  [from_group(): lax.ppermute(value, axis, [(i, i ^ k * stride) for i in range(count)])]
    ppermute x7, waiting for transfers between devices: 2.84 us -> 9.59 us  [from_group(): lax.ppermute(value, axis, [(i, i ^ k * stride) for i in range(count)])]
    ppermute x4, waiting for transfers between devices: 2.83 us -> 8.11 us  [from_neighbours(): lax.ppermute(high_edge, axis, forward)]
    ppermute x4, waiting for transfers between devices: 9.69 us -> 5.27 us  [from_neighbours(): lax.ppermute(low_edge, axis, backward)]
  transfers between devices with their start and end apart: 26 -> 26, of which waited for: 11 -> 11; matrix products, arithmetic and copies ran while one was open for 7% -> 7% of each run, Pallas kernels for 20% -> 15%
where the time goes in v2:
time: 210 us; the launch traced here: 207 us
  starting transfers between devices  76 us (36%)
  waiting for transfers between devices  62.8 us (30%)
  Pallas kernels  40.1 us (19%)
  local copies, waits for them, and re-layouts  22.9 us (11%)
  other arithmetic  4.65 us (2%)
    pallas_call x5, Pallas kernels, call(): pl.pallas_call(body, out_shape=outs, in_specs=specs, out_specs=out_specs,...  40.1 us
    ppermute x7, waiting for transfers between devices, to_members(): lax.ppermute(blocks[k], 'gy', [(i, i ^ k) for i in range(count)])  34.2 us
    ppermute x7, starting transfers between devices, from_group(): lax.ppermute(value, axis, [(i, i ^ k * stride) for i in range(count)])  26.4 us
    ppermute x3, starting transfers between devices, on_device(): lax.ppermute(wanted.astype(jnp.bfloat16), 'gx', [(i, i ^ k) for i in rang...  12.7 us
    ppermute x4, starting transfers between devices, from_neighbours(): lax.ppermute(low_edge, axis, backward)  12.2 us
    unnamed x49, local copies, waits for them, and re-layouts  12.1 us
    ppermute x7, starting transfers between devices, to_members(): lax.ppermute(blocks[k], 'gy', [(i, i ^ k) for i in range(count)])  10.7 us
    ppermute x7, waiting for transfers between devices, from_group(): lax.ppermute(value, axis, [(i, i ^ k * stride) for i in range(count)])  9.59 us
  transfers between devices with their start and end apart: 26, of which 11 were waited for; matrix products, arithmetic and copies ran while one was open for 7% of the time, Pallas kernels for 15%

profile of v2, /device:TPU:11, one launch (start us, length us, event | category | flops | bytes accessed | tf_op | source)
XLA Modules:
  0.0 207.5 jit_solution(1454683906648544299)
XLA Ops:
  2.0 1.1 slice_multiply_fusion.2
  3.1 3.1 %collective-permute-start = (bf16[8,1,96,128]{3,2,1,0:T(8,128)(2,1)S(1)}, bf16[8,1,96,128]{3,2,1,0:T(8,128)(2,1)S(1)}, u32[]{:S(2)}, u32[]{:S(2)}) collective-permute-start(bf16[8,1,96,128]{3,2,1,0:T(8,128)(2,1)S(1)} %get-tuple-element.62), channel_id=1, source_target_pairs={{0,1},{1,2},{2,3},{3,4},{4,5},{5,6},{6,7},{8,9},{9,10},{10,11},{11... | collective-permute-start | bytes 589832 | tf_op jit(solution)/shard_map/ppermute | solution.py:300
  6.2 3.0 %collective-permute-start.1 = (bf16[8,1,96,128]{3,2,1,0:T(8,128)(2,1)S(1)}, bf16[8,1,96,128]{3,2,1,0:T(8,128)(2,1)S(1)}, u32[]{:S(2)}, u32[]{:S(2)}) collective-permute-start(bf16[8,1,96,128]{3,2,1,0:T(8,128)(2,1)S(1)} %get-tuple-element.61), channel_id=1, source_target_pairs={{1,0},{2,1},{3,2},{4,3},{5,4},{6,5},{7,6},{9,8},{10,9},{11,10},{12... | collective-permute-start | bytes 589832 | tf_op jit(solution)/shard_map/ppermute | solution.py:300
  9.3 2.4 %collective-permute-done.y_low = bf16[8,1,96,128]{3,2,1,0:T(8,128)(2,1)S(1)} collective-permute-done((bf16[8,1,96,128]{3,2,1,0:T(8,128)(2,1)S(1)}, bf16[8,1,96,128]{3,2,1,0:T(8,128)(2,1)S(1)}, u32[]{:S(2)}, u32[]{:S(2)}) %collective-permute-start) | collective-permute-done | bytes 196640 | tf_op jit(solution)/shard_map/ppermute | solution.py:300
  11.6 5.3 %collective-permute-done.1.y_high = bf16[8,1,96,128]{3,2,1,0:T(8,128)(2,1)S(1)} collective-permute-done((bf16[8,1,96,128]{3,2,1,0:T(8,128)(2,1)S(1)}, bf16[8,1,96,128]{3,2,1,0:T(8,128)(2,1)S(1)}, u32[]{:S(2)}, u32[]{:S(2)}) %collective-permute-start.1) | collective-permute-done | bytes 196640 | tf_op jit(solution)/shard_map/ppermute | solution.py:300
  16.9 4.9 %all-to-all-start = ((bf16[8,384,512]{2,1,0:T(8,128)(2,1)}), bf16[8,384,512]{2,1,0:T(8,128)(2,1)S(1)}, u32[]{:S(2)}, u32[]{:S(2)}) async-start(bf16[8,384,512]{2,1,0:T(8,128)(2,1)} %bitcast.52), calls=%async_computation | async-start | bytes 6291456 | tf_op jit(solution)/shard_map/all_to_all | solution.py:365
  21.8 0.8 fusion.11
  22.6 1.1 slice_multiply_fusion
  24.4 1.3 collective-permute-start.2
  26.5 4.3 %collective-permute-start.3 = (bf16[1,10,96,128]{3,2,1,0:T(8,128)(2,1)}, bf16[1,10,96,128]{3,2,1,0:T(8,128)(2,1)}, u32[]{:S(2)}, u32[]{:S(2)}) collective-permute-start(bf16[1,10,96,128]{3,2,1,0:T(8,128)(2,1)} %pad_maximum_fusion.1), channel_id=1, source_target_pairs={{8,0},{16,8},{24,16},{9,1},{17,9},{25,17},{10,2},{18,10},{26,18},{... | collective-permute-start | bytes 737288 | tf_op jit(solution)/shard_map/ppermute | solution.py:300
  32.9 0.8 copy-done.5
  33.7 0.9 copy-done.7
  34.7 0.9 copy-done.9
  35.6 1.1 copy-done.11
  36.7 0.9 copy-done.21
  37.6 18.1 %shard_map.85 = (bf16[4,96,512]{2,1,0:T(8,128)(2,1)S(1)}, bf16[4,96,512]{2,1,0:T(8,128)(2,1)}, bf16[4,96,512]{2,1,0:T(8,128)(2,1)S(1)}, bf16[4,96,512]{2,1,0:T(8...) custom-call(s32[1]{0:T(128)} %bitcast.me_ref, ...), custom_call_target="tpu_custom_call" | custom-call | flops 4076863488 | bytes 11010048 | tf_op jit(solution)/shard_map/pallas_call | solution.py:279
  59.5 0.8 copy-done.18
  61.1 1.2 collective-permute-start.4
  62.6 1.2 collective-permute-start.6
  63.8 2.0 broadcast_in_dim.32
  66.6 8.0 %collective-permute-done.4 = bf16[4,96,512]{2,1,0:T(8,128)(2,1)} collective-permute-done((bf16[4,96,512]{2,1,0:T(8,128)(2,1)}, bf16[4,96,512]{2,1,0:T(8,128)(2,1)}, u32[]{:S(2)}, u32[]{:S(2)}) %collective-permute-start.4) | collective-permute-done | bytes 393248 | tf_op jit(solution)/shard_map/ppermute | solution.py:333
  74.6 1.8 bitcast_dynamic-update-slice_fusion.6
  76.4 6.1 %collective-permute-done.5 = bf16[4,96,512]{2,1,0:T(8,128)(2,1)S(1)} collective-permute-done((bf16[4,96,512]{2,1,0:T(8,128)(2,1)}, bf16[4,96,512]{2,1,0:T(8,128)(2,1)S(1)}, u32[]{:S(2)}, u32[]{:S(2)}) %collective-permute-start.5) | collective-permute-done | bytes 393248 | tf_op jit(solution)/shard_map/ppermute | solution.py:333
  83.3 8.2 %collective-permute-done.6 = bf16[4,96,512]{2,1,0:T(8,128)(2,1)S(1)} collective-permute-done((bf16[4,96,512]{2,1,0:T(8,128)(2,1)}, bf16[4,96,512]{2,1,0:T(8,128)(2,1)S(1)}, u32[]{:S(2)}, u32[]{:S(2)}) %collective-permute-start.6) | collective-permute-done | bytes 393248 | tf_op jit(solution)/shard_map/ppermute | solution.py:333
  92.2 1.6 collective-permute-start.7
  93.8 4.1 %collective-permute-start.8 = (bf16[4,96,512]{2,1,0:T(8,128)(2,1)}, bf16[4,96,512]{2,1,0:T(8,128)(2,1)S(1)}, u32[]{:S(2)}, u32[]{:S(2)}) collective-permute-start(bf16[4,96,512]{2,1,0:T(8,128)(2,1)} %copy-done.16), channel_id=1, source_target_pairs={{0,5},{1,4},{2,7},{3,6},{4,1},{5,0},{6,3},{7,2},{8,13},{9,12},{10,... | collective-permute-start | bytes 1179656 | tf_op jit(solution)/shard_map/ppermute | solution.py:333
  97.9 4.7 %shard_map.86.slope_ref = bf16[8,8,96,128]{3,2,1,0:T(8,128)(2,1)S(1)} custom-call(s32[1]{0:T(128)} %constant.52.clone.1.zero_ref, s32[16]{0:T(128)S(1)} %bitcast.50, bf16[32,96,512]{2,1,0:T(8,128)(2,1)S(1)} %bitcast.48, f32[8,8,96,128]{3,2,1,0:T(8,128)} %get-tuple-element.40.factor_ref), custom_call_target="tpu_custom_call" | custom-call | tf_op jit(solution)/shard_map/pallas_call | solution.py:279
  102.6 6.8 %shard_map.87 = f32[4,3,24,864]{3,2,1,0:T(8,128)S(1)} custom-call(bf16[8,8,96,128]{3,2,1,0:T(8,128)(2,1)S(1)} %shard_map.86.slope_ref, bf16[10,10,96,128]{3,2,1,0:T(8,128)(2,1)S(1)} %copy-done), custom_call_target="tpu_custom_call" | custom-call | tf_op jit(solution)/shard_map/pallas_call | solution.py:279
  109.6 11.9 %collective-permute-done.7 = bf16[4,96,512]{2,1,0:T(8,128)(2,1)S(1)} collective-permute-done((bf16[4,96,512]{2,1,0:T(8,128)(2,1)}, bf16[4,96,512]{2,1,0:T(8,128)(2,1)S(1)}, u32[]{:S(2)}, u32[]{:S(2)}) %collective-permute-start.7) | collective-permute-done | bytes 393248 | tf_op jit(solution)/shard_map/ppermute | solution.py:333
  121.6 10.0 %collective-permute-start.10 = (bf16[3,24,864]{2,1,0:T(8,128)(2,1)S(1)}, bf16[3,24,864]{2,1,0:T(8,128)(2,1)S(1)}, u32[]{:S(2)}, u32[]{:S(2)}) collective-permute-start(bf16[3,24,864]{2,1,0:T(8,128)(2,1)S(1)} %get-tuple-element.63), channel_id=1, source_target_pairs={{0,8},{8,0},{16,24},{24,16},{1,9},{9,1},{17,25},{25,17},{2,10},{10... | collective-permute-start | bytes 373256 | tf_op jit(solution)/shard_map/ppermute | solution.py:450
  131.6 2.3 %collective-permute-start.11 = (bf16[3,24,864]{2,1,0:T(8,128)(2,1)S(1)}, bf16[3,24,864]{2,1,0:T(8,128)(2,1)S(1)}, u32[]{:S(2)}, u32[]{:S(2)}) collective-permute-start(bf16[3,24,864]{2,1,0:T(8,128)(2,1)S(1)} %get-tuple-element.65), channel_id=1, source_target_pairs={{0,16},{8,24},{16,0},{24,8},{1,17},{9,25},{17,1},{25,9},{2,18},{10... | collective-permute-start | bytes 373256 | tf_op jit(solution)/shard_map/ppermute | solution.py:450
  135.0 2.3 %collective-permute-done.11 = bf16[3,24,864]{2,1,0:T(8,128)(2,1)S(1)} collective-permute-done((bf16[3,24,864]{2,1,0:T(8,128)(2,1)S(1)}, bf16[3,24,864]{2,1,0:T(8,128)(2,1)S(1)}, u32[]{:S(2)}, u32[]{:S(2)}) %collective-permute-start.11) | collective-permute-done | bytes 124448 | tf_op jit(solution)/shard_map/ppermute | solution.py:450
  137.4 3.3 %collective-permute-done.12 = bf16[3,24,864]{2,1,0:T(8,128)(2,1)S(1)} collective-permute-done((bf16[3,24,864]{2,1,0:T(8,128)(2,1)S(1)}, bf16[3,24,864]{2,1,0:T(8,128)(2,1)S(1)}, u32[]{:S(2)}, u32[]{:S(2)}) %collective-permute-start.12) | collective-permute-done | bytes 124448 | tf_op jit(solution)/shard_map/ppermute | solution.py:450
  140.9 0.8 bitcast_dynamic-update-slice_fusion.2
  141.7 2.3 %collective-permute-start.13 = (bf16[4,96,512]{2,1,0:T(8,128)(2,1)S(1)}, bf16[4,96,512]{2,1,0:T(8,128)(2,1)S(1)}, u32[]{:S(2)}, u32[]{:S(2)}) collective-permute-start(bf16[4,96,512]{2,1,0:T(8,128)(2,1)S(1)} %copy-done.13), channel_id=1, source_target_pairs={{0,7},{1,6},{2,5},{3,4},{4,3},{5,2},{6,1},{7,0},{8,15},{9,14},{10,... | collective-permute-start | bytes 1179656 | tf_op jit(solution)/shard_map/ppermute | solution.py:333
  144.0 3.3 %collective-permute-start.14 = (bf16[8,1,96,128]{3,2,1,0:T(8,128)(2,1)S(1)}, bf16[8,1,96,128]{3,2,1,0:T(8,128)(2,1)S(1)}, u32[]{:S(2)}, u32[]{:S(2)}) collective-permute-start(bf16[8,1,96,128]{3,2,1,0:T(8,128)(2,1)S(1)} %get-tuple-element.46), channel_id=1, source_target_pairs={{0,1},{1,2},{2,3},{3,4},{4,5},{5,6},{6,7},{8,9},{9,10},{10,11},{11... | collective-permute-start | bytes 589832 | tf_op jit(solution)/shard_map/ppermute | solution.py:300
  147.4 2.9 %collective-permute-start.15 = (bf16[8,1,96,128]{3,2,1,0:T(8,128)(2,1)S(1)}, bf16[8,1,96,128]{3,2,1,0:T(8,128)(2,1)S(1)}, u32[]{:S(2)}, u32[]{:S(2)}) collective-permute-start(bf16[8,1,96,128]{3,2,1,0:T(8,128)(2,1)S(1)} %get-tuple-element.47), channel_id=1, source_target_pairs={{1,0},{2,1},{3,2},{4,3},{5,4},{6,5},{7,6},{9,8},{10,9},{11,10},{12... | collective-permute-start | bytes 589832 | tf_op jit(solution)/shard_map/ppermute | solution.py:300
  150.4 3.6 %collective-permute-start.20 = (bf16[3,24,864]{2,1,0:T(8,128)(2,1)S(1)}, bf16[3,24,864]{2,1,0:T(8,128)(2,1)S(1)}, u32[]{:S(2)}, u32[]{:S(2)}) collective-permute-start(bf16[3,24,864]{2,1,0:T(8,128)(2,1)S(1)} %convert_add_fusion), channel_id=1, source_target_pairs={{0,4},{1,5},{2,6},{3,7},{4,0},{5,1},{6,2},{7,3},{8,12},{9,13},{10,... | collective-permute-start | bytes 373256 | tf_op jit(solution)/shard_map/ppermute | solution.py:325
  154.0 5.7 %collective-permute-done.14.y_low = bf16[8,1,96,128]{3,2,1,0:T(8,128)(2,1)S(1)} collective-permute-done((bf16[8,1,96,128]{3,2,1,0:T(8,128)(2,1)S(1)}, bf16[8,1,96,128]{3,2,1,0:T(8,128)(2,1)S(1)}, u32[]{:S(2)}, u32[]{:S(2)}) %collective-permute-start.14) | collective-permute-done | bytes 196640 | tf_op jit(solution)/shard_map/ppermute | solution.py:300
  159.7 14.9 %collective-permute-start.21 = (bf16[3,24,864]{2,1,0:T(8,128)(2,1)S(1)}, bf16[3,24,864]{2,1,0:T(8,128)(2,1)S(1)}, u32[]{:S(2)}, u32[]{:S(2)}) collective-permute-start(bf16[3,24,864]{2,1,0:T(8,128)(2,1)S(1)} %convert_add_fusion), channel_id=1, source_target_pairs={{0,6},{1,7},{2,4},{3,5},{4,2},{5,3},{6,0},{7,1},{8,14},{9,15},{10,... | collective-permute-start | bytes 373256 | tf_op jit(solution)/shard_map/ppermute | solution.py:325
  174.7 3.0 %collective-permute-done.21 = bf16[3,24,864]{2,1,0:T(8,128)(2,1)S(1)} collective-permute-done((bf16[3,24,864]{2,1,0:T(8,128)(2,1)S(1)}, bf16[3,24,864]{2,1,0:T(8,128)(2,1)S(1)}, u32[]{:S(2)}, u32[]{:S(2)}) %collective-permute-start.21) | collective-permute-done | bytes 124448 | tf_op jit(solution)/shard_map/ppermute | solution.py:325
  177.7 1.5 collective-permute-start.22
  179.3 1.9 collective-permute-start.17
  181.3 1.3 collective-permute-start.16
  182.6 6.0 %collective-permute-start.23 = (bf16[3,24,864]{2,1,0:T(8,128)(2,1)S(1)}, bf16[3,24,864]{2,1,0:T(8,128)(2,1)S(1)}, u32[]{:S(2)}, u32[]{:S(2)}) collective-permute-start(bf16[3,24,864]{2,1,0:T(8,128)(2,1)S(1)} %add_convert_fusion.refs_0_), channel_id=1, source_target_pairs={{0,16},{8,24},{16,0},{24,8},{1,17},{9,25},{17,1},{25,9},{2,18},{10... | collective-permute-start | bytes 373256 | tf_op jit(solution)/shard_map/ppermute | solution.py:325
  189.7 6.6 %collective-permute-done.23.refs_2_ = bf16[3,24,864]{2,1,0:T(8,128)(2,1)S(1)} collective-permute-done((bf16[3,24,864]{2,1,0:T(8,128)(2,1)S(1)}, bf16[3,24,864]{2,1,0:T(8,128)(2,1)S(1)}, u32[]{:S(2)}, u32[]{:S(2)}) %collective-permute-start.23) | collective-permute-done | bytes 124448 | tf_op jit(solution)/shard_map/ppermute | solution.py:325
  196.2 2.1 %shard_map.89 = f32[9,96,288]{2,1,0:T(8,128)} custom-call(s32[4]{0:T(128)S(1)} %pad_add_fusion.at_ref, bf16[3,24,864]{2,1,0:T(8,128)(2,1)S(1)} %add_convert_fusion.refs_0_, bf16[3,24,864]{2,1,0:T(8,128)(2,1)S(1)} %collective-permute-done.22.refs_1_, bf16[3,24,864]{2,1,0:T(8,128)(2,1)S(1)} %collective-permute-done.23.refs_2_, ...), custom_call_target="tpu_custom_call" | custom-call | flops 248832 | bytes 1492992 | tf_op jit(solution)/shard_map/pallas_call | solution.py:279
  199.1 8.4 %shard_map.88 = bf16[8,8,96,128]{3,2,1,0:T(8,128)(2,1)} custom-call(bf16[8,8,96,128]{3,2,1,0:T(8,128)(2,1)S(1)} %shard_map.86.slope_ref, s32[8,8,128]{2,1,0:T(8,128)S(1)} %copy-done.4, bf16[8,1,96,128]{3,2,1,0:T(8,128)(2,1)S(1)} %collective-permute-done.14.y_low, bf16[8,1,96,128]{3,2,1,0:T(8,128)(2,1)S(1)} %collective-permute-done.15.y_high, ...), custom_call_target="tpu_custom_call" | custom-call | tf_op jit(solution)/shard_map/pallas_call | solution.py:279
  (88 shorter events, 15.8 us)
Async XLA Ops:
  3.1 8.6 %collective-permute-start = (bf16[8,1,96,128]{3,2,1,0:T(8,128)(2,1)S(1)}, bf16[8,1,96,128]{3,2,1,0:T(8,128)(2,1)S(1)}, u32[]{:S(2)}, u32[]{:S(2)}) collective-permute-start(bf16[8,1,96,128]{3,2,1,0:T(8,128)(2,1)S(1)} %get-tuple-element.62), channel_id=1, source_target_pairs={{0,1},{1,2},{2,3},{3,4},{4,5},{5,6},{6,7},{8,9},{9,10},{10,11},{11... | collective-permute-start | bytes 589832 | tf_op jit(solution)/shard_map/ppermute | solution.py:300
  6.2 10.7 %collective-permute-start.1 = (bf16[8,1,96,128]{3,2,1,0:T(8,128)(2,1)S(1)}, bf16[8,1,96,128]{3,2,1,0:T(8,128)(2,1)S(1)}, u32[]{:S(2)}, u32[]{:S(2)}) collective-permute-start(bf16[8,1,96,128]{3,2,1,0:T(8,128)(2,1)S(1)} %get-tuple-element.61), channel_id=1, source_target_pairs={{1,0},{2,1},{3,2},{4,3},{5,4},{6,5},{7,6},{9,8},{10,9},{11,10},{12... | collective-permute-start | bytes 589832 | tf_op jit(solution)/shard_map/ppermute | solution.py:300
  11.6 12.0 %copy-start.6 = (bf16[8,1,96,128]{3,2,1,0:T(8,128)(2,1)}, bf16[8,1,96,128]{3,2,1,0:T(8,128)(2,1)S(1)}, u32[]{:S(2)}) copy-start(bf16[8,1,96,128]{3,2,1,0:T(8,128)(2,1)S(1)} %collective-permute-done.y_low) | copy-start | bytes 589828
  16.9 6.8 %copy-start.8 = (bf16[8,1,96,128]{3,2,1,0:T(8,128)(2,1)}, bf16[8,1,96,128]{3,2,1,0:T(8,128)(2,1)S(1)}, u32[]{:S(2)}) copy-start(bf16[8,1,96,128]{3,2,1,0:T(8,128)(2,1)S(1)} %collective-permute-done.1.y_high) | copy-start | bytes 589828
  16.9 13.9 %copy-start.23 = (f32[96]{0:T(128)S(1)}, f32[96]{0:T(128)}, u32[]{:S(2)}) copy-start(f32[96]{0:T(128)} %param.10) | copy-start | bytes 1156
  16.9 15.3 %copy-start.10 = (s32[1,1,16]{2,1,0:T(1,128)S(1)}, s32[1,1,16]{2,1,0:T(1,128)}, u32[]{:S(2)}) copy-start(s32[1,1,16]{2,1,0:T(1,128)} %param.8) | copy-start | bytes 196
  16.9 75.3 %all-to-all-start = ((bf16[8,384,512]{2,1,0:T(8,128)(2,1)}), bf16[8,384,512]{2,1,0:T(8,128)(2,1)S(1)}, u32[]{:S(2)}, u32[]{:S(2)}) async-start(bf16[8,384,512]{2,1,0:T(8,128)(2,1)} %bitcast.52), calls=%async_computation | async-start | bytes 6291456 | tf_op jit(solution)/shard_map/all_to_all | solution.py:365
  24.4 7.0 %collective-permute-start.2 = (bf16[1,10,96,128]{3,2,1,0:T(8,128)(2,1)}, bf16[1,10,96,128]{3,2,1,0:T(8,128)(2,1)S(1)}, u32[]{:S(2)}, u32[]{:S(2)}) collective-permute-start(bf16[1,10,96,128]{3,2,1,0:T(8,128)(2,1)} %pad_maximum_fusion), channel_id=1, source_target_pairs={{0,8},{8,16},{16,24},{1,9},{9,17},{17,25},{2,10},{10,18},{18,26},{... | collective-permute-start | bytes 737288 | tf_op jit(solution)/shard_map/ppermute | solution.py:300
  26.5 5.7 %collective-permute-start.3 = (bf16[1,10,96,128]{3,2,1,0:T(8,128)(2,1)}, bf16[1,10,96,128]{3,2,1,0:T(8,128)(2,1)}, u32[]{:S(2)}, u32[]{:S(2)}) collective-permute-start(bf16[1,10,96,128]{3,2,1,0:T(8,128)(2,1)} %pad_maximum_fusion.1), channel_id=1, source_target_pairs={{8,0},{16,8},{24,16},{9,1},{17,9},{25,17},{10,2},{18,10},{26,18},{... | collective-permute-start | bytes 737288 | tf_op jit(solution)/shard_map/ppermute | solution.py:300
  32.2 0.8 copy-start.3
  32.9 0.8 copy-start.5
  33.7 0.9 copy-start.7
  34.7 0.9 copy-start.9
  35.6 1.1 copy-start.11
  36.7 0.9 copy-start.21
  55.7 0.8 copy-start.1
  56.5 0.7 copy-start.12
  57.3 0.7 copy-start.14
  58.0 0.8 copy-start.16
  58.8 0.8 copy-start.17
  59.5 0.8 copy-start.18
  60.3 0.8 copy-start.19
  61.1 13.6 %collective-permute-start.4 = (bf16[4,96,512]{2,1,0:T(8,128)(2,1)}, bf16[4,96,512]{2,1,0:T(8,128)(2,1)}, u32[]{:S(2)}, u32[]{:S(2)}) collective-permute-start(bf16[4,96,512]{2,1,0:T(8,128)(2,1)} %get-tuple-element.30), channel_id=1, source_target_pairs={{0,1},{1,0},{2,3},{3,2},{4,5},{5,4},{6,7},{7,6},{8,9},{9,8},{10,11... | collective-permute-start | bytes 1179656 | tf_op jit(solution)/shard_map/ppermute | solution.py:333
  62.3 20.2 %collective-permute-start.5 = (bf16[4,96,512]{2,1,0:T(8,128)(2,1)}, bf16[4,96,512]{2,1,0:T(8,128)(2,1)S(1)}, u32[]{:S(2)}, u32[]{:S(2)}) collective-permute-start(bf16[4,96,512]{2,1,0:T(8,128)(2,1)} %copy-done.19), channel_id=1, source_target_pairs={{0,2},{1,3},{2,0},{3,1},{4,6},{5,7},{6,4},{7,5},{8,10},{9,11},{10,... | collective-permute-start | bytes 1179656 | tf_op jit(solution)/shard_map/ppermute | solution.py:333
  62.6 28.8 %collective-permute-start.6 = (bf16[4,96,512]{2,1,0:T(8,128)(2,1)}, bf16[4,96,512]{2,1,0:T(8,128)(2,1)S(1)}, u32[]{:S(2)}, u32[]{:S(2)}) collective-permute-start(bf16[4,96,512]{2,1,0:T(8,128)(2,1)} %copy-done.18), channel_id=1, source_target_pairs={{0,3},{1,2},{2,1},{3,0},{4,7},{5,6},{6,5},{7,4},{8,11},{9,10},{10,... | collective-permute-start | bytes 1179656 | tf_op jit(solution)/shard_map/ppermute | solution.py:333
  92.2 29.3 %collective-permute-start.7 = (bf16[4,96,512]{2,1,0:T(8,128)(2,1)}, bf16[4,96,512]{2,1,0:T(8,128)(2,1)S(1)}, u32[]{:S(2)}, u32[]{:S(2)}) collective-permute-start(bf16[4,96,512]{2,1,0:T(8,128)(2,1)} %copy-done.17), channel_id=1, source_target_pairs={{0,4},{1,5},{2,6},{3,7},{4,0},{5,1},{6,2},{7,3},{8,12},{9,13},{10,... | collective-permute-start | bytes 1179656 | tf_op jit(solution)/shard_map/ppermute | solution.py:333
  93.8 47.0 %collective-permute-start.8 = (bf16[4,96,512]{2,1,0:T(8,128)(2,1)}, bf16[4,96,512]{2,1,0:T(8,128)(2,1)S(1)}, u32[]{:S(2)}, u32[]{:S(2)}) collective-permute-start(bf16[4,96,512]{2,1,0:T(8,128)(2,1)} %copy-done.16), channel_id=1, source_target_pairs={{0,5},{1,4},{2,7},{3,6},{4,1},{5,0},{6,3},{7,2},{8,13},{9,12},{10,... | collective-permute-start | bytes 1179656 | tf_op jit(solution)/shard_map/ppermute | solution.py:333
  97.9 4.7 %copy-start = (bf16[10,10,96,128]{3,2,1,0:T(8,128)(2,1)S(1)}, bf16[10,10,96,128]{3,2,1,0:T(8,128)(2,1)}, u32[]{:S(2)}) copy-start(bf16[10,10,96,128]{3,2,1,0:T(8,128)(2,1)} %get-tuple-element.41.padded_ref) | copy-start | bytes 7372804
  102.6 6.9 %copy-start.15 = (bf16[4,96,512]{2,1,0:T(8,128)(2,1)S(1)}, bf16[4,96,512]{2,1,0:T(8,128)(2,1)}, u32[]{:S(2)}) copy-start(bf16[4,96,512]{2,1,0:T(8,128)(2,1)} %copy-done.14) | copy-start | bytes 1179652
  109.5 32.2 %copy-start.13 = (bf16[4,96,512]{2,1,0:T(8,128)(2,1)S(1)}, bf16[4,96,512]{2,1,0:T(8,128)(2,1)}, u32[]{:S(2)}) copy-start(bf16[4,96,512]{2,1,0:T(8,128)(2,1)} %copy-done.12) | copy-start | bytes 1179652
  109.5 40.9 %collective-permute-start.9 = (bf16[4,96,512]{2,1,0:T(8,128)(2,1)S(1)}, bf16[4,96,512]{2,1,0:T(8,128)(2,1)S(1)}, u32[]{:S(2)}, u32[]{:S(2)}) collective-permute-start(bf16[4,96,512]{2,1,0:T(8,128)(2,1)S(1)} %copy-done.15), channel_id=1, source_target_pairs={{0,6},{1,7},{2,4},{3,5},{4,2},{5,3},{6,0},{7,1},{8,14},{9,15},{10,... | collective-permute-start | bytes 1179656 | tf_op jit(solution)/shard_map/ppermute | solution.py:333
  121.6 13.5 %collective-permute-start.10 = (bf16[3,24,864]{2,1,0:T(8,128)(2,1)S(1)}, bf16[3,24,864]{2,1,0:T(8,128)(2,1)S(1)}, u32[]{:S(2)}, u32[]{:S(2)}) collective-permute-start(bf16[3,24,864]{2,1,0:T(8,128)(2,1)S(1)} %get-tuple-element.63), channel_id=1, source_target_pairs={{0,8},{8,0},{16,24},{24,16},{1,9},{9,1},{17,25},{25,17},{2,10},{10... | collective-permute-start | bytes 373256 | tf_op jit(solution)/shard_map/ppermute | solution.py:450
  131.6 5.8 %collective-permute-start.11 = (bf16[3,24,864]{2,1,0:T(8,128)(2,1)S(1)}, bf16[3,24,864]{2,1,0:T(8,128)(2,1)S(1)}, u32[]{:S(2)}, u32[]{:S(2)}) collective-permute-start(bf16[3,24,864]{2,1,0:T(8,128)(2,1)S(1)} %get-tuple-element.65), channel_id=1, source_target_pairs={{0,16},{8,24},{16,0},{24,8},{1,17},{9,25},{17,1},{25,9},{2,18},{10... | collective-permute-start | bytes 373256 | tf_op jit(solution)/shard_map/ppermute | solution.py:450
  133.9 6.8 %collective-permute-start.12 = (bf16[3,24,864]{2,1,0:T(8,128)(2,1)S(1)}, bf16[3,24,864]{2,1,0:T(8,128)(2,1)S(1)}, u32[]{:S(2)}, u32[]{:S(2)}) collective-permute-start(bf16[3,24,864]{2,1,0:T(8,128)(2,1)S(1)} %get-tuple-element.64), channel_id=1, source_target_pairs={{0,24},{8,16},{16,8},{24,0},{1,25},{9,17},{17,9},{25,1},{2,26},{10... | collective-permute-start | bytes 373256 | tf_op jit(solution)/shard_map/ppermute | solution.py:450
  140.8 58.4 %copy-start.2 = (bf16[288,864]{1,0:T(8,128)(2,1)S(1)}, bf16[288,864]{1,0:T(8,128)(2,1)}, u32[]{:S(2)}) copy-start(bf16[288,864]{1,0:T(8,128)(2,1)} %copy-done.1) | copy-start | bytes 1492996
  140.8 58.4 %copy-start.4 = (s32[8,8,128]{2,1,0:T(8,128)S(1)}, s32[8,8,128]{2,1,0:T(8,128)}, u32[]{:S(2)}) copy-start(s32[8,8,128]{2,1,0:T(8,128)} %mask_ref.3) | copy-start | bytes 98308
  140.8 9.5 %collective-permute-start.18 = (bf16[3,24,864]{2,1,0:T(8,128)(2,1)S(1)}, bf16[3,24,864]{2,1,0:T(8,128)(2,1)S(1)}, u32[]{:S(2)}, u32[]{:S(2)}) collective-permute-start(bf16[3,24,864]{2,1,0:T(8,128)(2,1)S(1)} %fusion.1), channel_id=1, source_target_pairs={{0,1},{1,0},{2,3},{3,2},{4,5},{5,4},{6,7},{7,6},{8,9},{9,8},{10,11... | collective-permute-start | bytes 373256 | tf_op jit(solution)/shard_map/ppermute | solution.py:325
  141.7 54.6 %collective-permute-start.13 = (bf16[4,96,512]{2,1,0:T(8,128)(2,1)S(1)}, bf16[4,96,512]{2,1,0:T(8,128)(2,1)S(1)}, u32[]{:S(2)}, u32[]{:S(2)}) collective-permute-start(bf16[4,96,512]{2,1,0:T(8,128)(2,1)S(1)} %copy-done.13), channel_id=1, source_target_pairs={{0,7},{1,6},{2,5},{3,4},{4,3},{5,2},{6,1},{7,0},{8,15},{9,14},{10,... | collective-permute-start | bytes 1179656 | tf_op jit(solution)/shard_map/ppermute | solution.py:333
  144.0 15.7 %collective-permute-start.14 = (bf16[8,1,96,128]{3,2,1,0:T(8,128)(2,1)S(1)}, bf16[8,1,96,128]{3,2,1,0:T(8,128)(2,1)S(1)}, u32[]{:S(2)}, u32[]{:S(2)}) collective-permute-start(bf16[8,1,96,128]{3,2,1,0:T(8,128)(2,1)S(1)} %get-tuple-element.46), channel_id=1, source_target_pairs={{0,1},{1,2},{2,3},{3,4},{4,5},{5,6},{6,7},{8,9},{9,10},{10,11},{11... | collective-permute-start | bytes 589832 | tf_op jit(solution)/shard_map/ppermute | solution.py:300
  147.4 27.3 %collective-permute-start.15 = (bf16[8,1,96,128]{3,2,1,0:T(8,128)(2,1)S(1)}, bf16[8,1,96,128]{3,2,1,0:T(8,128)(2,1)S(1)}, u32[]{:S(2)}, u32[]{:S(2)}) collective-permute-start(bf16[8,1,96,128]{3,2,1,0:T(8,128)(2,1)S(1)} %get-tuple-element.47), channel_id=1, source_target_pairs={{1,0},{2,1},{3,2},{4,3},{5,4},{6,5},{7,6},{9,8},{10,9},{11,10},{12... | collective-permute-start | bytes 589832 | tf_op jit(solution)/shard_map/ppermute | solution.py:300
  150.3 24.3 %collective-permute-start.19 = (bf16[3,24,864]{2,1,0:T(8,128)(2,1)S(1)}, bf16[3,24,864]{2,1,0:T(8,128)(2,1)S(1)}, u32[]{:S(2)}, u32[]{:S(2)}) collective-permute-start(bf16[3,24,864]{2,1,0:T(8,128)(2,1)S(1)} %convert_add_fusion), channel_id=1, source_target_pairs={{0,2},{1,3},{2,0},{3,1},{4,6},{5,7},{6,4},{7,5},{8,10},{9,11},{10,... | collective-permute-start | bytes 373256 | tf_op jit(solution)/shard_map/ppermute | solution.py:325
  150.4 24.2 %collective-permute-start.20 = (bf16[3,24,864]{2,1,0:T(8,128)(2,1)S(1)}, bf16[3,24,864]{2,1,0:T(8,128)(2,1)S(1)}, u32[]{:S(2)}, u32[]{:S(2)}) collective-permute-start(bf16[3,24,864]{2,1,0:T(8,128)(2,1)S(1)} %convert_add_fusion), channel_id=1, source_target_pairs={{0,4},{1,5},{2,6},{3,7},{4,0},{5,1},{6,2},{7,3},{8,12},{9,13},{10,... | collective-permute-start | bytes 373256 | tf_op jit(solution)/shard_map/ppermute | solution.py:325
  159.7 17.9 %collective-permute-start.21 = (bf16[3,24,864]{2,1,0:T(8,128)(2,1)S(1)}, bf16[3,24,864]{2,1,0:T(8,128)(2,1)S(1)}, u32[]{:S(2)}, u32[]{:S(2)}) collective-permute-start(bf16[3,24,864]{2,1,0:T(8,128)(2,1)S(1)} %convert_add_fusion), channel_id=1, source_target_pairs={{0,6},{1,7},{2,4},{3,5},{4,2},{5,3},{6,0},{7,1},{8,14},{9,15},{10,... | collective-permute-start | bytes 373256 | tf_op jit(solution)/shard_map/ppermute | solution.py:325
  177.7 10.9 %collective-permute-start.22 = (bf16[3,24,864]{2,1,0:T(8,128)(2,1)S(1)}, bf16[3,24,864]{2,1,0:T(8,128)(2,1)S(1)}, u32[]{:S(2)}, u32[]{:S(2)}) collective-permute-start(bf16[3,24,864]{2,1,0:T(8,128)(2,1)S(1)} %add_convert_fusion.refs_0_), channel_id=1, source_target_pairs={{0,8},{8,0},{16,24},{24,16},{1,9},{9,1},{17,25},{25,17},{2,10},{10... | collective-permute-start | bytes 373256 | tf_op jit(solution)/shard_map/ppermute | solution.py:325
  179.3 19.8 %collective-permute-start.17 = (bf16[1,10,96,128]{3,2,1,0:T(8,128)(2,1)S(1)}, bf16[1,10,96,128]{3,2,1,0:T(8,128)(2,1)S(1)}, u32[]{:S(2)}, u32[]{:S(2)}) collective-permute-start(bf16[1,10,96,128]{3,2,1,0:T(8,128)(2,1)S(1)} %pad_maximum_fusion.3), channel_id=1, source_target_pairs={{8,0},{16,8},{24,16},{9,1},{17,9},{25,17},{10,2},{18,10},{26,18},{... | collective-permute-start | bytes 737288 | tf_op jit(solution)/shard_map/ppermute | solution.py:300
  181.3 17.8 %collective-permute-start.16 = (bf16[1,10,96,128]{3,2,1,0:T(8,128)(2,1)S(1)}, bf16[1,10,96,128]{3,2,1,0:T(8,128)(2,1)S(1)}, u32[]{:S(2)}, u32[]{:S(2)}) collective-permute-start(bf16[1,10,96,128]{3,2,1,0:T(8,128)(2,1)S(1)} %pad_maximum_fusion.2), channel_id=1, source_target_pairs={{0,8},{8,16},{16,24},{1,9},{9,17},{17,25},{2,10},{10,18},{18,26},{... | collective-permute-start | bytes 737288 | tf_op jit(solution)/shard_map/ppermute | solution.py:300
  182.6 13.6 %collective-permute-start.23 = (bf16[3,24,864]{2,1,0:T(8,128)(2,1)S(1)}, bf16[3,24,864]{2,1,0:T(8,128)(2,1)S(1)}, u32[]{:S(2)}, u32[]{:S(2)}) collective-permute-start(bf16[3,24,864]{2,1,0:T(8,128)(2,1)S(1)} %add_convert_fusion.refs_0_), channel_id=1, source_target_pairs={{0,16},{8,24},{16,0},{24,8},{1,17},{9,25},{17,1},{25,9},{2,18},{10... | collective-permute-start | bytes 373256 | tf_op jit(solution)/shard_map/ppermute | solution.py:325
  188.6 7.6 %collective-permute-start.24 = (bf16[3,24,864]{2,1,0:T(8,128)(2,1)S(1)}, bf16[3,24,864]{2,1,0:T(8,128)(2,1)S(1)}, u32[]{:S(2)}, u32[]{:S(2)}) collective-permute-start(bf16[3,24,864]{2,1,0:T(8,128)(2,1)S(1)} %add_convert_fusion.refs_0_), channel_id=1, source_target_pairs={{0,24},{8,16},{16,8},{24,0},{1,25},{9,17},{17,9},{25,1},{2,26},{10... | collective-permute-start | bytes 373256 | tf_op jit(solution)/shard_map/ppermute | solution.py:325
  (2 other events, 1.3 us)

commit v3 on v1

--- a/solution.py
+++ b/solution.py
@@ -451,7 +451,7 @@
             wanted.astype(jnp.bfloat16), "gx", [(i, i ^ k) for i in range(members_x)]
         ).astype(jnp.float32)
     columns = [edge_of(slope)(side, False) for side in (0, -1)]
-    slope_halo = from_neighbours(*after(columns, total), "gy")
+    slope_halo = from_neighbours(*after(columns, shares), "gy")
     for index, (radix, stride) in enumerate(((members // 4, 1), (4, members // 4))):
         total = in_turn(total, index + 1)
         sent = total.astype(jnp.bfloat16)

time: 191 us -> 202 us (1.058); the launches traced: 190 us -> 199 us
  waiting for transfers between devices: 55.2 us -> 65.8 us
    ppermute x7, waiting for transfers between devices: 2.84 us -> 17.4 us  [from_group(): lax.ppermute(value, axis, [(i, i ^ k * stride) for i in range(count)])]
    ppermute x3, waiting for transfers between devices: 5.66 us -> 0.01 us  [on_device(): lax.ppermute(wanted.astype(jnp.bfloat16), 'gx', [(i, i ^ k) for i in rang...]
    ppermute x7, starting transfers between devices: 15.1 us -> 12.5 us  [from_group(): lax.ppermute(value, axis, [(i, i ^ k * stride) for i in range(count)])]
    ppermute x4, waiting for transfers between devices: 9.69 us -> 11.8 us  [from_neighbours(): lax.ppermute(low_edge, axis, backward)]
  transfers between devices with their start and end apart: 26 -> 26, of which waited for: 11 -> 9; matrix products, arithmetic and copies ran while one was open for 7% -> 6% of each run, Pallas kernels for 20% -> 19%
where the time goes in v3:
time: 202 us; the launch traced here: 199 us
  waiting for transfers between devices  65.8 us (33%)
  starting transfers between devices  64.2 us (32%)
  Pallas kernels  40.1 us (20%)
  local copies, waits for them, and re-layouts  22.9 us (11%)
  other arithmetic  4.65 us (2%)
    pallas_call x5, Pallas kernels, call(): pl.pallas_call(body, out_shape=outs, in_specs=specs, out_specs=out_specs,...  40.1 us
    ppermute x7, waiting for transfers between devices, to_members(): lax.ppermute(blocks[k], 'gy', [(i, i ^ k) for i in range(count)])  34.2 us
    ppermute x7, waiting for transfers between devices, from_group(): lax.ppermute(value, axis, [(i, i ^ k * stride) for i in range(count)])  17.4 us
    ppermute x4, starting transfers between devices, from_neighbours(): lax.ppermute(low_edge, axis, backward)  14.4 us
    ppermute x3, starting transfers between devices, on_device(): lax.ppermute(wanted.astype(jnp.bfloat16), 'gx', [(i, i ^ k) for i in rang...  12.7 us
    ppermute x7, starting transfers between devices, from_group(): lax.ppermute(value, axis, [(i, i ^ k * stride) for i in range(count)])  12.5 us
    unnamed x49, local copies, waits for them, and re-layouts  12.1 us
    ppermute x4, waiting for transfers between devices, from_neighbours(): lax.ppermute(low_edge, axis, backward)  11.8 us
  transfers between devices with their start and end apart: 26, of which 9 were waited for; matrix products, arithmetic and copies ran while one was open for 6% of the time, Pallas kernels for 19%

profile of v3, /device:TPU:11, one launch (start us, length us, event | category | flops | bytes accessed | tf_op | source)
XLA Modules:
  0.0 198.7 jit_solution(6988639668257818677)
XLA Ops:
  2.0 1.1 slice_multiply_fusion.2
  3.1 3.1 %collective-permute-start = (bf16[8,1,96,128]{3,2,1,0:T(8,128)(2,1)S(1)}, bf16[8,1,96,128]{3,2,1,0:T(8,128)(2,1)S(1)}, u32[]{:S(2)}, u32[]{:S(2)}) collective-permute-start(bf16[8,1,96,128]{3,2,1,0:T(8,128)(2,1)S(1)} %get-tuple-element.62), channel_id=1, source_target_pairs={{0,1},{1,2},{2,3},{3,4},{4,5},{5,6},{6,7},{8,9},{9,10},{10,11},{11... | collective-permute-start | bytes 589832 | tf_op jit(solution)/shard_map/ppermute | solution.py:300
  6.2 3.0 %collective-permute-start.1 = (bf16[8,1,96,128]{3,2,1,0:T(8,128)(2,1)S(1)}, bf16[8,1,96,128]{3,2,1,0:T(8,128)(2,1)S(1)}, u32[]{:S(2)}, u32[]{:S(2)}) collective-permute-start(bf16[8,1,96,128]{3,2,1,0:T(8,128)(2,1)S(1)} %get-tuple-element.61), channel_id=1, source_target_pairs={{1,0},{2,1},{3,2},{4,3},{5,4},{6,5},{7,6},{9,8},{10,9},{11,10},{12... | collective-permute-start | bytes 589832 | tf_op jit(solution)/shard_map/ppermute | solution.py:300
  9.3 2.4 %collective-permute-done.y_low = bf16[8,1,96,128]{3,2,1,0:T(8,128)(2,1)S(1)} collective-permute-done((bf16[8,1,96,128]{3,2,1,0:T(8,128)(2,1)S(1)}, bf16[8,1,96,128]{3,2,1,0:T(8,128)(2,1)S(1)}, u32[]{:S(2)}, u32[]{:S(2)}) %collective-permute-start) | collective-permute-done | bytes 196640 | tf_op jit(solution)/shard_map/ppermute | solution.py:300
  11.6 5.3 %collective-permute-done.1.y_high = bf16[8,1,96,128]{3,2,1,0:T(8,128)(2,1)S(1)} collective-permute-done((bf16[8,1,96,128]{3,2,1,0:T(8,128)(2,1)S(1)}, bf16[8,1,96,128]{3,2,1,0:T(8,128)(2,1)S(1)}, u32[]{:S(2)}, u32[]{:S(2)}) %collective-permute-start.1) | collective-permute-done | bytes 196640 | tf_op jit(solution)/shard_map/ppermute | solution.py:300
  16.9 4.9 %all-to-all-start = ((bf16[8,384,512]{2,1,0:T(8,128)(2,1)}), bf16[8,384,512]{2,1,0:T(8,128)(2,1)S(1)}, u32[]{:S(2)}, u32[]{:S(2)}) async-start(bf16[8,384,512]{2,1,0:T(8,128)(2,1)} %bitcast.52), calls=%async_computation | async-start | bytes 6291456 | tf_op jit(solution)/shard_map/all_to_all | solution.py:365
  21.8 0.8 fusion.11
  22.6 1.1 slice_multiply_fusion
  24.4 1.3 collective-permute-start.2
  26.5 4.3 %collective-permute-start.3 = (bf16[1,10,96,128]{3,2,1,0:T(8,128)(2,1)}, bf16[1,10,96,128]{3,2,1,0:T(8,128)(2,1)}, u32[]{:S(2)}, u32[]{:S(2)}) collective-permute-start(bf16[1,10,96,128]{3,2,1,0:T(8,128)(2,1)} %pad_maximum_fusion.1), channel_id=1, source_target_pairs={{8,0},{16,8},{24,16},{9,1},{17,9},{25,17},{10,2},{18,10},{26,18},{... | collective-permute-start | bytes 737288 | tf_op jit(solution)/shard_map/ppermute | solution.py:300
  32.2 0.8 copy-done.1
  33.7 0.9 copy-done.5
  34.7 0.9 copy-done.7
  35.6 1.1 copy-done.9
  36.7 0.9 copy-done.19
  37.6 18.1 %shard_map.85 = (bf16[4,96,512]{2,1,0:T(8,128)(2,1)S(1)}, bf16[4,96,512]{2,1,0:T(8,128)(2,1)}, bf16[4,96,512]{2,1,0:T(8,128)(2,1)S(1)}, bf16[4,96,512]{2,1,0:T(8...) custom-call(s32[1]{0:T(128)} %bitcast.me_ref, ...), custom_call_target="tpu_custom_call" | custom-call | flops 4076863488 | bytes 11010048 | tf_op jit(solution)/shard_map/pallas_call | solution.py:279
  58.7 0.8 copy-done.16
  60.3 0.8 copy-done.20
  61.1 1.2 collective-permute-start.4
  62.6 1.2 collective-permute-start.6
  63.8 2.0 %broadcast_in_dim.32 = bf16[8,4,96,512]{3,2,1,0:T(8,128)(2,1)} broadcast(bf16[]{:T(256)} %constant.43.clone.1), dimensions={} | broadcast | bytes 3145730 | tf_op jit(solution)/shard_map/broadcast_in_dim | solution.py:493
  66.6 8.0 %collective-permute-done.4 = bf16[4,96,512]{2,1,0:T(8,128)(2,1)} collective-permute-done((bf16[4,96,512]{2,1,0:T(8,128)(2,1)}, bf16[4,96,512]{2,1,0:T(8,128)(2,1)}, u32[]{:S(2)}, u32[]{:S(2)}) %collective-permute-start.4) | collective-permute-done | bytes 393248 | tf_op jit(solution)/shard_map/ppermute | solution.py:333
  74.6 1.8 bitcast_dynamic-update-slice_fusion.6
  76.4 6.1 %collective-permute-done.5 = bf16[4,96,512]{2,1,0:T(8,128)(2,1)S(1)} collective-permute-done((bf16[4,96,512]{2,1,0:T(8,128)(2,1)}, bf16[4,96,512]{2,1,0:T(8,128)(2,1)S(1)}, u32[]{:S(2)}, u32[]{:S(2)}) %collective-permute-start.5) | collective-permute-done | bytes 393248 | tf_op jit(solution)/shard_map/ppermute | solution.py:333
  82.5 0.8 bitcast_dynamic-update-slice_fusion.5
  83.3 8.2 %collective-permute-done.6 = bf16[4,96,512]{2,1,0:T(8,128)(2,1)S(1)} collective-permute-done((bf16[4,96,512]{2,1,0:T(8,128)(2,1)}, bf16[4,96,512]{2,1,0:T(8,128)(2,1)S(1)}, u32[]{:S(2)}, u32[]{:S(2)}) %collective-permute-start.6) | collective-permute-done | bytes 393248 | tf_op jit(solution)/shard_map/ppermute | solution.py:333
  91.5 0.8 bitcast_dynamic-update-slice_fusion.4
  92.2 1.6 collective-permute-start.7
  93.8 4.1 %collective-permute-start.8 = (bf16[4,96,512]{2,1,0:T(8,128)(2,1)}, bf16[4,96,512]{2,1,0:T(8,128)(2,1)S(1)}, u32[]{:S(2)}, u32[]{:S(2)}) collective-permute-start(bf16[4,96,512]{2,1,0:T(8,128)(2,1)} %copy-done.14), channel_id=1, source_target_pairs={{0,5},{1,4},{2,7},{3,6},{4,1},{5,0},{6,3},{7,2},{8,13},{9,12},{10,... | collective-permute-start | bytes 1179656 | tf_op jit(solution)/shard_map/ppermute | solution.py:333
  97.9 4.7 %shard_map.86.slope_ref = bf16[8,8,96,128]{3,2,1,0:T(8,128)(2,1)S(1)} custom-call(s32[1]{0:T(128)} %constant.52.clone.1.zero_ref, s32[16]{0:T(128)S(1)} %bitcast.50, bf16[32,96,512]{2,1,0:T(8,128)(2,1)S(1)} %bitcast.48, f32[8,8,96,128]{3,2,1,0:T(8,128)} %get-tuple-element.40.factor_ref), custom_call_target="tpu_custom_call" | custom-call | tf_op jit(solution)/shard_map/pallas_call | solution.py:279
  102.7 6.8 %shard_map.87 = f32[4,3,24,864]{3,2,1,0:T(8,128)S(1)} custom-call(bf16[8,8,96,128]{3,2,1,0:T(8,128)(2,1)S(1)} %shard_map.86.slope_ref, bf16[10,10,96,128]{3,2,1,0:T(8,128)(2,1)S(1)} %copy-done), custom_call_target="tpu_custom_call" | custom-call | tf_op jit(solution)/shard_map/pallas_call | solution.py:279
  109.7 11.8 %collective-permute-done.7 = bf16[4,96,512]{2,1,0:T(8,128)(2,1)S(1)} collective-permute-done((bf16[4,96,512]{2,1,0:T(8,128)(2,1)}, bf16[4,96,512]{2,1,0:T(8,128)(2,1)S(1)}, u32[]{:S(2)}, u32[]{:S(2)}) %collective-permute-start.7) | collective-permute-done | bytes 393248 | tf_op jit(solution)/shard_map/ppermute | solution.py:333
  121.6 10.0 %collective-permute-start.10 = (bf16[3,24,864]{2,1,0:T(8,128)(2,1)S(1)}, bf16[3,24,864]{2,1,0:T(8,128)(2,1)S(1)}, u32[]{:S(2)}, u32[]{:S(2)}) collective-permute-start(bf16[3,24,864]{2,1,0:T(8,128)(2,1)S(1)} %get-tuple-element.63), channel_id=1, source_target_pairs={{0,8},{8,0},{16,24},{24,16},{1,9},{9,1},{17,25},{25,17},{2,10},{10... | collective-permute-start | bytes 373256 | tf_op jit(solution)/shard_map/ppermute | solution.py:450
  131.6 2.3 %collective-permute-start.11 = (bf16[3,24,864]{2,1,0:T(8,128)(2,1)S(1)}, bf16[3,24,864]{2,1,0:T(8,128)(2,1)S(1)}, u32[]{:S(2)}, u32[]{:S(2)}) collective-permute-start(bf16[3,24,864]{2,1,0:T(8,128)(2,1)S(1)} %get-tuple-element.65), channel_id=1, source_target_pairs={{0,16},{8,24},{16,0},{24,8},{1,17},{9,25},{17,1},{25,9},{2,18},{10... | collective-permute-start | bytes 373256 | tf_op jit(solution)/shard_map/ppermute | solution.py:450
  135.0 4.8 %collective-permute-start.15 = (bf16[8,1,96,128]{3,2,1,0:T(8,128)(2,1)S(1)}, bf16[8,1,96,128]{3,2,1,0:T(8,128)(2,1)S(1)}, u32[]{:S(2)}, u32[]{:S(2)}) collective-permute-start(bf16[8,1,96,128]{3,2,1,0:T(8,128)(2,1)S(1)} %get-tuple-element.47), channel_id=1, source_target_pairs={{0,1},{1,2},{2,3},{3,4},{4,5},{5,6},{6,7},{8,9},{9,10},{10,11},{11... | collective-permute-start | bytes 589832 | tf_op jit(solution)/shard_map/ppermute | solution.py:300
  139.8 0.8 bitcast_dynamic-update-slice_fusion.2
  140.6 3.2 %collective-permute-start.16 = (bf16[8,1,96,128]{3,2,1,0:T(8,128)(2,1)S(1)}, bf16[8,1,96,128]{3,2,1,0:T(8,128)(2,1)S(1)}, u32[]{:S(2)}, u32[]{:S(2)}) collective-permute-start(bf16[8,1,96,128]{3,2,1,0:T(8,128)(2,1)S(1)} %get-tuple-element.48), channel_id=1, source_target_pairs={{1,0},{2,1},{3,2},{4,3},{5,4},{6,5},{7,6},{9,8},{10,9},{11,10},{12... | collective-permute-start | bytes 589832 | tf_op jit(solution)/shard_map/ppermute | solution.py:300
  144.2 6.6 %collective-permute-done.16.y_high = bf16[8,1,96,128]{3,2,1,0:T(8,128)(2,1)S(1)} collective-permute-done((bf16[8,1,96,128]{3,2,1,0:T(8,128)(2,1)S(1)}, bf16[8,1,96,128]{3,2,1,0:T(8,128)(2,1)S(1)}, u32[]{:S(2)}, u32[]{:S(2)}) %collective-permute-start.16) | collective-permute-done | bytes 196640 | tf_op jit(solution)/shard_map/ppermute | solution.py:300
  150.8 3.9 %collective-permute-start.18 = (bf16[1,10,96,128]{3,2,1,0:T(8,128)(2,1)S(1)}, bf16[1,10,96,128]{3,2,1,0:T(8,128)(2,1)S(1)}, u32[]{:S(2)}, u32[]{:S(2)}) collective-permute-start(bf16[1,10,96,128]{3,2,1,0:T(8,128)(2,1)S(1)} %pad_maximum_fusion.3), channel_id=1, source_target_pairs={{8,0},{16,8},{24,16},{9,1},{17,9},{25,17},{10,2},{18,10},{26,18},{... | collective-permute-start | bytes 737288 | tf_op jit(solution)/shard_map/ppermute | solution.py:300
  154.7 1.3 collective-permute-start.17
  156.7 5.1 %collective-permute-start.20 = (bf16[3,24,864]{2,1,0:T(8,128)(2,1)S(1)}, bf16[3,24,864]{2,1,0:T(8,128)(2,1)S(1)}, u32[]{:S(2)}, u32[]{:S(2)}) collective-permute-start(bf16[3,24,864]{2,1,0:T(8,128)(2,1)S(1)} %convert_add_fusion), channel_id=1, source_target_pairs={{0,4},{1,5},{2,6},{3,7},{4,0},{5,1},{6,2},{7,3},{8,12},{9,13},{10,... | collective-permute-start | bytes 373256 | tf_op jit(solution)/shard_map/ppermute | solution.py:325
  162.7 0.8 collective-permute-start.14
  163.5 2.2 %collective-permute-done.20 = bf16[3,24,864]{2,1,0:T(8,128)(2,1)S(1)} collective-permute-done((bf16[3,24,864]{2,1,0:T(8,128)(2,1)S(1)}, bf16[3,24,864]{2,1,0:T(8,128)(2,1)S(1)}, u32[]{:S(2)}, u32[]{:S(2)}) %collective-permute-start.20) | collective-permute-done | bytes 124448 | tf_op jit(solution)/shard_map/ppermute | solution.py:325
  165.7 15.1 %collective-permute-done.21 = bf16[3,24,864]{2,1,0:T(8,128)(2,1)S(1)} collective-permute-done((bf16[3,24,864]{2,1,0:T(8,128)(2,1)S(1)}, bf16[3,24,864]{2,1,0:T(8,128)(2,1)S(1)}, u32[]{:S(2)}, u32[]{:S(2)}) %collective-permute-start.21) | collective-permute-done | bytes 124448 | tf_op jit(solution)/shard_map/ppermute | solution.py:325
  180.9 3.7 %collective-permute-start.22 = (bf16[3,24,864]{2,1,0:T(8,128)(2,1)S(1)}, bf16[3,24,864]{2,1,0:T(8,128)(2,1)S(1)}, u32[]{:S(2)}, u32[]{:S(2)}) collective-permute-start(bf16[3,24,864]{2,1,0:T(8,128)(2,1)S(1)} %add_convert_fusion.refs_0_), channel_id=1, source_target_pairs={{0,8},{8,0},{16,24},{24,16},{1,9},{9,1},{17,25},{25,17},{2,10},{10... | collective-permute-start | bytes 373256 | tf_op jit(solution)/shard_map/ppermute | solution.py:325
  184.6 2.7 %collective-permute-start.23 = (bf16[3,24,864]{2,1,0:T(8,128)(2,1)S(1)}, bf16[3,24,864]{2,1,0:T(8,128)(2,1)S(1)}, u32[]{:S(2)}, u32[]{:S(2)}) collective-permute-start(bf16[3,24,864]{2,1,0:T(8,128)(2,1)S(1)} %add_convert_fusion.refs_0_), channel_id=1, source_target_pairs={{0,16},{8,24},{16,0},{24,8},{1,17},{9,25},{17,1},{25,9},{2,18},{10... | collective-permute-start | bytes 373256 | tf_op jit(solution)/shard_map/ppermute | solution.py:325
  187.4 8.4 %shard_map.88 = bf16[8,8,96,128]{3,2,1,0:T(8,128)(2,1)} custom-call(bf16[8,8,96,128]{3,2,1,0:T(8,128)(2,1)S(1)} %shard_map.86.slope_ref, s32[8,8,128]{2,1,0:T(8,128)S(1)} %copy-done.3, bf16[8,1,96,128]{3,2,1,0:T(8,128)(2,1)S(1)} %collective-permute-done.15.y_low, bf16[8,1,96,128]{3,2,1,0:T(8,128)(2,1)S(1)} %collective-permute-done.16.y_high, ...), custom_call_target="tpu_custom_call" | custom-call | flops 4076863488 | bytes 3932160 | tf_op jit(solution)/shard_map/pallas_call | solution.py:279
  195.8 2.1 %shard_map.89 = f32[9,96,288]{2,1,0:T(8,128)} custom-call(s32[4]{0:T(128)S(1)} %pad_add_fusion.at_ref, bf16[3,24,864]{2,1,0:T(8,128)(2,1)S(1)} %add_convert_fusion.refs_0_, bf16[3,24,864]{2,1,0:T(8,128)(2,1)S(1)} %collective-permute-done.22.refs_1_, bf16[3,24,864]{2,1,0:T(8,128)(2,1)S(1)} %collective-permute-done.23.refs_2_, ...), custom_call_target="tpu_custom_call" | custom-call | flops 248832 | bytes 1492992 | tf_op jit(solution)/shard_map/pallas_call | solution.py:279
  (88 shorter events, 14.0 us)
Async XLA Ops:
  3.1 8.6 %collective-permute-start = (bf16[8,1,96,128]{3,2,1,0:T(8,128)(2,1)S(1)}, bf16[8,1,96,128]{3,2,1,0:T(8,128)(2,1)S(1)}, u32[]{:S(2)}, u32[]{:S(2)}) collective-permute-start(bf16[8,1,96,128]{3,2,1,0:T(8,128)(2,1)S(1)} %get-tuple-element.62), channel_id=1, source_target_pairs={{0,1},{1,2},{2,3},{3,4},{4,5},{5,6},{6,7},{8,9},{9,10},{10,11},{11... | collective-permute-start | bytes 589832 | tf_op jit(solution)/shard_map/ppermute | solution.py:300
  6.2 10.7 %collective-permute-start.1 = (bf16[8,1,96,128]{3,2,1,0:T(8,128)(2,1)S(1)}, bf16[8,1,96,128]{3,2,1,0:T(8,128)(2,1)S(1)}, u32[]{:S(2)}, u32[]{:S(2)}) collective-permute-start(bf16[8,1,96,128]{3,2,1,0:T(8,128)(2,1)S(1)} %get-tuple-element.61), channel_id=1, source_target_pairs={{1,0},{2,1},{3,2},{4,3},{5,4},{6,5},{7,6},{9,8},{10,9},{11,10},{12... | collective-permute-start | bytes 589832 | tf_op jit(solution)/shard_map/ppermute | solution.py:300
  11.6 12.0 %copy-start.4 = (bf16[8,1,96,128]{3,2,1,0:T(8,128)(2,1)}, bf16[8,1,96,128]{3,2,1,0:T(8,128)(2,1)S(1)}, u32[]{:S(2)}) copy-start(bf16[8,1,96,128]{3,2,1,0:T(8,128)(2,1)S(1)} %collective-permute-done.y_low) | copy-start | bytes 589828
  16.9 6.8 %copy-start.6 = (bf16[8,1,96,128]{3,2,1,0:T(8,128)(2,1)}, bf16[8,1,96,128]{3,2,1,0:T(8,128)(2,1)S(1)}, u32[]{:S(2)}) copy-start(bf16[8,1,96,128]{3,2,1,0:T(8,128)(2,1)S(1)} %collective-permute-done.1.y_high) | copy-start | bytes 589828
  16.9 13.9 %copy-start.23 = (f32[96]{0:T(128)S(1)}, f32[96]{0:T(128)}, u32[]{:S(2)}) copy-start(f32[96]{0:T(128)} %param.10) | copy-start | bytes 1156
  16.9 15.3 %copy-start.8 = (s32[1,1,16]{2,1,0:T(1,128)S(1)}, s32[1,1,16]{2,1,0:T(1,128)}, u32[]{:S(2)}) copy-start(s32[1,1,16]{2,1,0:T(1,128)} %param.8) | copy-start | bytes 196
  16.9 75.3 %all-to-all-start = ((bf16[8,384,512]{2,1,0:T(8,128)(2,1)}), bf16[8,384,512]{2,1,0:T(8,128)(2,1)S(1)}, u32[]{:S(2)}, u32[]{:S(2)}) async-start(bf16[8,384,512]{2,1,0:T(8,128)(2,1)} %bitcast.52), calls=%async_computation | async-start | bytes 6291456 | tf_op jit(solution)/shard_map/all_to_all | solution.py:365
  24.4 7.0 %collective-permute-start.2 = (bf16[1,10,96,128]{3,2,1,0:T(8,128)(2,1)}, bf16[1,10,96,128]{3,2,1,0:T(8,128)(2,1)S(1)}, u32[]{:S(2)}, u32[]{:S(2)}) collective-permute-start(bf16[1,10,96,128]{3,2,1,0:T(8,128)(2,1)} %pad_maximum_fusion), channel_id=1, source_target_pairs={{0,8},{8,16},{16,24},{1,9},{9,17},{17,25},{2,10},{10,18},{18,26},{... | collective-permute-start | bytes 737288 | tf_op jit(solution)/shard_map/ppermute | solution.py:300
  26.5 5.7 %collective-permute-start.3 = (bf16[1,10,96,128]{3,2,1,0:T(8,128)(2,1)}, bf16[1,10,96,128]{3,2,1,0:T(8,128)(2,1)}, u32[]{:S(2)}, u32[]{:S(2)}) collective-permute-start(bf16[1,10,96,128]{3,2,1,0:T(8,128)(2,1)} %pad_maximum_fusion.1), channel_id=1, source_target_pairs={{8,0},{16,8},{24,16},{9,1},{17,9},{25,17},{10,2},{18,10},{26,18},{... | collective-permute-start | bytes 737288 | tf_op jit(solution)/shard_map/ppermute | solution.py:300
  32.2 0.8 copy-start.1
  33.0 0.8 copy-start.2
  33.7 0.9 copy-start.5
  34.7 0.9 copy-start.7
  35.6 1.1 copy-start.9
  36.7 0.9 copy-start.19
  55.7 0.7 copy-start.10
  56.5 0.7 copy-start.12
  57.2 0.8 copy-start.14
  58.0 0.8 copy-start.15
  58.7 0.8 copy-start.16
  59.5 0.8 copy-start.17
  60.3 0.8 copy-start.20
  61.1 13.6 %collective-permute-start.4 = (bf16[4,96,512]{2,1,0:T(8,128)(2,1)}, bf16[4,96,512]{2,1,0:T(8,128)(2,1)}, u32[]{:S(2)}, u32[]{:S(2)}) collective-permute-start(bf16[4,96,512]{2,1,0:T(8,128)(2,1)} %get-tuple-element.30), channel_id=1, source_target_pairs={{0,1},{1,0},{2,3},{3,2},{4,5},{5,4},{6,7},{7,6},{8,9},{9,8},{10,11... | collective-permute-start | bytes 1179656 | tf_op jit(solution)/shard_map/ppermute | solution.py:333
  62.3 20.2 %collective-permute-start.5 = (bf16[4,96,512]{2,1,0:T(8,128)(2,1)}, bf16[4,96,512]{2,1,0:T(8,128)(2,1)S(1)}, u32[]{:S(2)}, u32[]{:S(2)}) collective-permute-start(bf16[4,96,512]{2,1,0:T(8,128)(2,1)} %copy-done.17), channel_id=1, source_target_pairs={{0,2},{1,3},{2,0},{3,1},{4,6},{5,7},{6,4},{7,5},{8,10},{9,11},{10,... | collective-permute-start | bytes 1179656 | tf_op jit(solution)/shard_map/ppermute | solution.py:333
  62.6 28.8 %collective-permute-start.6 = (bf16[4,96,512]{2,1,0:T(8,128)(2,1)}, bf16[4,96,512]{2,1,0:T(8,128)(2,1)S(1)}, u32[]{:S(2)}, u32[]{:S(2)}) collective-permute-start(bf16[4,96,512]{2,1,0:T(8,128)(2,1)} %copy-done.16), channel_id=1, source_target_pairs={{0,3},{1,2},{2,1},{3,0},{4,7},{5,6},{6,5},{7,4},{8,11},{9,10},{10,... | collective-permute-start | bytes 1179656 | tf_op jit(solution)/shard_map/ppermute | solution.py:333
  92.2 29.3 %collective-permute-start.7 = (bf16[4,96,512]{2,1,0:T(8,128)(2,1)}, bf16[4,96,512]{2,1,0:T(8,128)(2,1)S(1)}, u32[]{:S(2)}, u32[]{:S(2)}) collective-permute-start(bf16[4,96,512]{2,1,0:T(8,128)(2,1)} %copy-done.15), channel_id=1, source_target_pairs={{0,4},{1,5},{2,6},{3,7},{4,0},{5,1},{6,2},{7,3},{8,12},{9,13},{10,... | collective-permute-start | bytes 1179656 | tf_op jit(solution)/shard_map/ppermute | solution.py:333
  93.8 41.2 %collective-permute-start.8 = (bf16[4,96,512]{2,1,0:T(8,128)(2,1)}, bf16[4,96,512]{2,1,0:T(8,128)(2,1)S(1)}, u32[]{:S(2)}, u32[]{:S(2)}) collective-permute-start(bf16[4,96,512]{2,1,0:T(8,128)(2,1)} %copy-done.14), channel_id=1, source_target_pairs={{0,5},{1,4},{2,7},{3,6},{4,1},{5,0},{6,3},{7,2},{8,13},{9,12},{10,... | collective-permute-start | bytes 1179656 | tf_op jit(solution)/shard_map/ppermute | solution.py:333
  97.9 4.8 %copy-start = (bf16[10,10,96,128]{3,2,1,0:T(8,128)(2,1)S(1)}, bf16[10,10,96,128]{3,2,1,0:T(8,128)(2,1)}, u32[]{:S(2)}) copy-start(bf16[10,10,96,128]{3,2,1,0:T(8,128)(2,1)} %get-tuple-element.41.padded_ref) | copy-start | bytes 7372804
  102.6 7.0 %copy-start.13 = (bf16[4,96,512]{2,1,0:T(8,128)(2,1)S(1)}, bf16[4,96,512]{2,1,0:T(8,128)(2,1)}, u32[]{:S(2)}) copy-start(bf16[4,96,512]{2,1,0:T(8,128)(2,1)} %copy-done.12) | copy-start | bytes 1179652
  109.5 53.1 %copy-start.11 = (bf16[4,96,512]{2,1,0:T(8,128)(2,1)S(1)}, bf16[4,96,512]{2,1,0:T(8,128)(2,1)}, u32[]{:S(2)}) copy-start(bf16[4,96,512]{2,1,0:T(8,128)(2,1)} %copy-done.10) | copy-start | bytes 1179652
  109.5 77.8 %copy-start.3 = (s32[8,8,128]{2,1,0:T(8,128)S(1)}, s32[8,8,128]{2,1,0:T(8,128)}, u32[]{:S(2)}) copy-start(s32[8,8,128]{2,1,0:T(8,128)} %mask_ref.3) | copy-start | bytes 98308
  109.6 77.8 %copy-start.21 = (bf16[288,864]{1,0:T(8,128)(2,1)S(1)}, bf16[288,864]{1,0:T(8,128)(2,1)}, u32[]{:S(2)}) copy-start(bf16[288,864]{1,0:T(8,128)(2,1)} %copy-done.20) | copy-start | bytes 1492996
  109.6 46.5 %collective-permute-start.9 = (bf16[4,96,512]{2,1,0:T(8,128)(2,1)S(1)}, bf16[4,96,512]{2,1,0:T(8,128)(2,1)S(1)}, u32[]{:S(2)}, u32[]{:S(2)}) collective-permute-start(bf16[4,96,512]{2,1,0:T(8,128)(2,1)S(1)} %copy-done.13), channel_id=1, source_target_pairs={{0,6},{1,7},{2,4},{3,5},{4,2},{5,3},{6,0},{7,1},{8,14},{9,15},{10,... | collective-permute-start | bytes 1179656 | tf_op jit(solution)/shard_map/ppermute | solution.py:333
  121.6 19.1 %collective-permute-start.10 = (bf16[3,24,864]{2,1,0:T(8,128)(2,1)S(1)}, bf16[3,24,864]{2,1,0:T(8,128)(2,1)S(1)}, u32[]{:S(2)}, u32[]{:S(2)}) collective-permute-start(bf16[3,24,864]{2,1,0:T(8,128)(2,1)S(1)} %get-tuple-element.63), channel_id=1, source_target_pairs={{0,8},{8,0},{16,24},{24,16},{1,9},{9,1},{17,25},{25,17},{2,10},{10... | collective-permute-start | bytes 373256 | tf_op jit(solution)/shard_map/ppermute | solution.py:450
  131.6 12.2 %collective-permute-start.11 = (bf16[3,24,864]{2,1,0:T(8,128)(2,1)S(1)}, bf16[3,24,864]{2,1,0:T(8,128)(2,1)S(1)}, u32[]{:S(2)}, u32[]{:S(2)}) collective-permute-start(bf16[3,24,864]{2,1,0:T(8,128)(2,1)S(1)} %get-tuple-element.65), channel_id=1, source_target_pairs={{0,16},{8,24},{16,0},{24,8},{1,17},{9,25},{17,1},{25,9},{2,18},{10... | collective-permute-start | bytes 373256 | tf_op jit(solution)/shard_map/ppermute | solution.py:450
  133.9 9.9 %collective-permute-start.12 = (bf16[3,24,864]{2,1,0:T(8,128)(2,1)S(1)}, bf16[3,24,864]{2,1,0:T(8,128)(2,1)S(1)}, u32[]{:S(2)}, u32[]{:S(2)}) collective-permute-start(bf16[3,24,864]{2,1,0:T(8,128)(2,1)S(1)} %get-tuple-element.64), channel_id=1, source_target_pairs={{0,24},{8,16},{16,8},{24,0},{1,25},{9,17},{17,9},{25,1},{2,26},{10... | collective-permute-start | bytes 373256 | tf_op jit(solution)/shard_map/ppermute | solution.py:450
  135.0 9.1 %collective-permute-start.15 = (bf16[8,1,96,128]{3,2,1,0:T(8,128)(2,1)S(1)}, bf16[8,1,96,128]{3,2,1,0:T(8,128)(2,1)S(1)}, u32[]{:S(2)}, u32[]{:S(2)}) collective-permute-start(bf16[8,1,96,128]{3,2,1,0:T(8,128)(2,1)S(1)} %get-tuple-element.47), channel_id=1, source_target_pairs={{0,1},{1,2},{2,3},{3,4},{4,5},{5,6},{6,7},{8,9},{9,10},{10,11},{11... | collective-permute-start | bytes 589832 | tf_op jit(solution)/shard_map/ppermute | solution.py:300
  140.6 10.1 %collective-permute-start.16 = (bf16[8,1,96,128]{3,2,1,0:T(8,128)(2,1)S(1)}, bf16[8,1,96,128]{3,2,1,0:T(8,128)(2,1)S(1)}, u32[]{:S(2)}, u32[]{:S(2)}) collective-permute-start(bf16[8,1,96,128]{3,2,1,0:T(8,128)(2,1)S(1)} %get-tuple-element.48), channel_id=1, source_target_pairs={{1,0},{2,1},{3,2},{4,3},{5,4},{6,5},{7,6},{9,8},{10,9},{11,10},{12... | collective-permute-start | bytes 589832 | tf_op jit(solution)/shard_map/ppermute | solution.py:300
  143.9 12.1 %collective-permute-start.13 = (bf16[3,24,864]{2,1,0:T(8,128)(2,1)S(1)}, bf16[3,24,864]{2,1,0:T(8,128)(2,1)S(1)}, u32[]{:S(2)}, u32[]{:S(2)}) collective-permute-start(bf16[3,24,864]{2,1,0:T(8,128)(2,1)S(1)} %fusion.1), channel_id=1, source_target_pairs={{0,1},{1,0},{2,3},{3,2},{4,5},{5,4},{6,7},{7,6},{8,9},{9,8},{10,11... | collective-permute-start | bytes 373256 | tf_op jit(solution)/shard_map/ppermute | solution.py:325
  150.8 36.6 %collective-permute-start.18 = (bf16[1,10,96,128]{3,2,1,0:T(8,128)(2,1)S(1)}, bf16[1,10,96,128]{3,2,1,0:T(8,128)(2,1)S(1)}, u32[]{:S(2)}, u32[]{:S(2)}) collective-permute-start(bf16[1,10,96,128]{3,2,1,0:T(8,128)(2,1)S(1)} %pad_maximum_fusion.3), channel_id=1, source_target_pairs={{8,0},{16,8},{24,16},{9,1},{17,9},{25,17},{10,2},{18,10},{26,18},{... | collective-permute-start | bytes 737288 | tf_op jit(solution)/shard_map/ppermute | solution.py:300
  154.7 32.7 %collective-permute-start.17 = (bf16[1,10,96,128]{3,2,1,0:T(8,128)(2,1)S(1)}, bf16[1,10,96,128]{3,2,1,0:T(8,128)(2,1)S(1)}, u32[]{:S(2)}, u32[]{:S(2)}) collective-permute-start(bf16[1,10,96,128]{3,2,1,0:T(8,128)(2,1)S(1)} %pad_maximum_fusion.2), channel_id=1, source_target_pairs={{0,8},{8,16},{16,24},{1,9},{9,17},{17,25},{2,10},{10,18},{18,26},{... | collective-permute-start | bytes 737288 | tf_op jit(solution)/shard_map/ppermute | solution.py:300
  156.1 6.6 %collective-permute-start.19 = (bf16[3,24,864]{2,1,0:T(8,128)(2,1)S(1)}, bf16[3,24,864]{2,1,0:T(8,128)(2,1)S(1)}, u32[]{:S(2)}, u32[]{:S(2)}) collective-permute-start(bf16[3,24,864]{2,1,0:T(8,128)(2,1)S(1)} %convert_add_fusion), channel_id=1, source_target_pairs={{0,2},{1,3},{2,0},{3,1},{4,6},{5,7},{6,4},{7,5},{8,10},{9,11},{10,... | collective-permute-start | bytes 373256 | tf_op jit(solution)/shard_map/ppermute | solution.py:325
  156.7 9.0 %collective-permute-start.20 = (bf16[3,24,864]{2,1,0:T(8,128)(2,1)S(1)}, bf16[3,24,864]{2,1,0:T(8,128)(2,1)S(1)}, u32[]{:S(2)}, u32[]{:S(2)}) collective-permute-start(bf16[3,24,864]{2,1,0:T(8,128)(2,1)S(1)} %convert_add_fusion), channel_id=1, source_target_pairs={{0,4},{1,5},{2,6},{3,7},{4,0},{5,1},{6,2},{7,3},{8,12},{9,13},{10,... | collective-permute-start | bytes 373256 | tf_op jit(solution)/shard_map/ppermute | solution.py:325
  161.9 19.0 %collective-permute-start.21 = (bf16[3,24,864]{2,1,0:T(8,128)(2,1)S(1)}, bf16[3,24,864]{2,1,0:T(8,128)(2,1)S(1)}, u32[]{:S(2)}, u32[]{:S(2)}) collective-permute-start(bf16[3,24,864]{2,1,0:T(8,128)(2,1)S(1)} %convert_add_fusion), channel_id=1, source_target_pairs={{0,6},{1,7},{2,4},{3,5},{4,2},{5,3},{6,0},{7,1},{8,14},{9,15},{10,... | collective-permute-start | bytes 373256 | tf_op jit(solution)/shard_map/ppermute | solution.py:325
  162.7 33.1 %collective-permute-start.14 = (bf16[4,96,512]{2,1,0:T(8,128)(2,1)S(1)}, bf16[4,96,512]{2,1,0:T(8,128)(2,1)S(1)}, u32[]{:S(2)}, u32[]{:S(2)}) collective-permute-start(bf16[4,96,512]{2,1,0:T(8,128)(2,1)S(1)} %copy-done.11), channel_id=1, source_target_pairs={{0,7},{1,6},{2,5},{3,4},{4,3},{5,2},{6,1},{7,0},{8,15},{9,14},{10,... | collective-permute-start | bytes 1179656 | tf_op jit(solution)/shard_map/ppermute | solution.py:333
  180.9 14.9 %collective-permute-start.22 = (bf16[3,24,864]{2,1,0:T(8,128)(2,1)S(1)}, bf16[3,24,864]{2,1,0:T(8,128)(2,1)S(1)}, u32[]{:S(2)}, u32[]{:S(2)}) collective-permute-start(bf16[3,24,864]{2,1,0:T(8,128)(2,1)S(1)} %add_convert_fusion.refs_0_), channel_id=1, source_target_pairs={{0,8},{8,0},{16,24},{24,16},{1,9},{9,1},{17,25},{25,17},{2,10},{10... | collective-permute-start | bytes 373256 | tf_op jit(solution)/shard_map/ppermute | solution.py:325
  184.6 11.2 %collective-permute-start.23 = (bf16[3,24,864]{2,1,0:T(8,128)(2,1)S(1)}, bf16[3,24,864]{2,1,0:T(8,128)(2,1)S(1)}, u32[]{:S(2)}, u32[]{:S(2)}) collective-permute-start(bf16[3,24,864]{2,1,0:T(8,128)(2,1)S(1)} %add_convert_fusion.refs_0_), channel_id=1, source_target_pairs={{0,16},{8,24},{16,0},{24,8},{1,17},{9,25},{17,1},{25,9},{2,18},{10... | collective-permute-start | bytes 373256 | tf_op jit(solution)/shard_map/ppermute | solution.py:325
  187.3 8.5 %collective-permute-start.24 = (bf16[3,24,864]{2,1,0:T(8,128)(2,1)S(1)}, bf16[3,24,864]{2,1,0:T(8,128)(2,1)S(1)}, u32[]{:S(2)}, u32[]{:S(2)}) collective-permute-start(bf16[3,24,864]{2,1,0:T(8,128)(2,1)S(1)} %add_convert_fusion.refs_0_), channel_id=1, source_target_pairs={{0,24},{8,16},{16,8},{24,0},{1,25},{9,17},{17,9},{25,1},{2,26},{10... | collective-permute-start | bytes 373256 | tf_op jit(solution)/shard_map/ppermute | solution.py:325
  (2 other events, 1.3 us)
